TPU v7x, 32 devices: a whole 2x2x4 slice. The times are simulated.
32 devices in a mesh: groups: 2 (over y), expert: 4 (over z), tensor: 2 (over x), dp: 2 (over core).
Axes of the slice: x: 2, y: 2, z: 4, core: 2. Of those that a mesh axis runs over, the one named last changes fastest.
Arguments:
- inputs: bfloat16 [2, 256, 3584], P(None, ('groups', 'expert', 'dp')), parts along dimension 1, may hold values from -6 to 6
- attn_gain: float32 [3584], replicated, may hold values from 0.1 to 1.9
- qkv_weight: bfloat16 [3584, 512], P('tensor'), may hold values from -0.09375 to 0.09375
- out_weight: bfloat16 [256, 3584], P(None, 'tensor'), may hold values from -0.375 to 0.375
- cache: bfloat16 [256, 256, 256], P(('groups', 'expert', 'dp'), 'tensor'), parts along dimension 0, may hold values from -240 to 240
- lengths: int32 [256], P(('groups', 'expert', 'dp')), parts along dimension 0, may hold values from 1 to 256, as said below
- moe_gain: float32 [3584], replicated, may hold values from 0.1 to 1.9
- router_weight: bfloat16 [3584, 16], replicated, may hold values from -0.09375 to 0.09375
- expert_ids: int32 [2, 256, 8], P(None, ('groups', 'expert', 'dp')), parts along dimension 1, may hold values from 0 to 15, all different within a row; in each aligned block of 16 rows (0 to 15, 16 to 31, ..., all dimensions but the last counted through in order) at most 15 rows name the same one
- gate_weight: bfloat16 [16, 3584, 1024], P('expert', 'tensor'), may hold values from -0.09375 to 0.09375
- up_weight: bfloat16 [16, 3584, 1024], P('expert', 'tensor'), may hold values from -0.09375 to 0.09375
- down_weight: bfloat16 [16, 1024, 3584], P('expert', None, 'tensor'), may hold values from -0.1875 to 0.1875
- pool_left: bfloat16 [64, 2, 3584, 64], P(('groups', 'expert'), None, 'tensor'), parts along dimension 0, may hold values from -0.75 to 0.75
- pool_right: bfloat16 [64, 2, 64, 1024], P(('groups', 'expert'), None, None, 'dp'), parts along dimension 0, may hold values from -0.09375 to 0.09375
- pair_slot: int32 [32], P('groups'), parts along dimension 0, may hold values from 0 to 31, as said below
Outputs:
- outputs: bfloat16 [2, 256, 3584], P(None, ('groups', 'expert', 'dp'), 'tensor'), parts along dimension 1
There are 2 independent parts, one for each index of `groups`. A program takes and returns all parts, laid end to end along the dimension named above; an argument that names none is the same for every part. Nothing has to cross between parts.
Inputs may be any that keep to these rules, and one draw needn't show every extreme that they name: `expert_ids`: each row names 8 different experts; in the rows of one device at one step (aligned blocks of 16 rows) no expert is named by more than 15 rows, a bound that some block reaches. `pair_slot`: slot j lies on trainer shard j // 8; no slot holds two experts; some trainer shard holds 8 experts. `lengths`: some row has length 256.
All inputs are finite; a program needn't handle non-finite values.
Results may differ from a plain program's by a relative error of at most 0.015.
The roundings to bfloat16 on the way count: a program that leaves them out, or rounds other values in their place, can miss the bound.
Values may be sent and summed in bfloat16 or wider, within the bound.
A program may use at most 192 MiB of HBM per device.

v0:
```python
import jax
import jax.numpy as jnp
from jax import lax
from jax.sharding import PartitionSpec as P

D = 3584
LAT = 256
EXPERTS = 16
STEPS = 2
CAP = 15


EPS = 1e-06
ROUTE_SCALE = 2.5
FLOOR = -1e30


def merged_2(value, axis, join):
    pieces = jax.tree.map(lambda part: lax.all_gather(part, axis), value)
    head = jax.tree.map(lambda part: part[0], pieces)
    tail = jax.tree.map(lambda part: part[1:], pieces)
    subtotal, _ = lax.scan(lambda subtotal, slab: (join(subtotal, slab), None), head, tail)
    return subtotal


def normalized(values, norm_gain):
    widened = values.astype(jnp.float32)
    square_mean = jnp.mean(widened * widened, axis=-1, keepdims=True)
    return (widened * lax.rsqrt(square_mean + EPS) * norm_gain).astype(jnp.bfloat16)


def softmax_join(earlier, following):
    highest = jnp.maximum(earlier[0], following[0])
    early_factor = jnp.exp(earlier[0] - highest)
    late_factor = jnp.exp(following[0] - highest)
    return (
        highest,
        earlier[1] * early_factor + following[1] * late_factor,
        earlier[2] * early_factor[:, None] + following[2] * late_factor[:, None],
    )


def shards(
    inputs,
    attn_gain,
    qkv_weight,
    out_weight,
    cache,
    lengths,
    moe_gain,
    router_weight,
    expert_ids,
    gate_weight,
    up_weight,
    down_weight,
    pool_left,
    pool_right,
    pair_slot,
):
    experts_here = gate_weight.shape[0]
    part_cols = gate_weight.shape[1]
    shard_count = lax.axis_size("expert")
    shard_index = lax.axis_index("expert")
    col_start = lax.axis_index("tensor") * part_cols
    span_here = cache.shape[1]
    rows_here = inputs.shape[1]
    score_scale = LAT ** (-0.5)
    wanted = jnp.take(
        pair_slot, shard_index * experts_here + jnp.arange(experts_here, dtype=jnp.int32), axis=0
    )
    pieces = (
        lax.all_gather(pool_left, "expert", axis=0, tiled=True),
        lax.all_gather(pool_right, "expert", axis=0, tiled=True),
    )
    piece_count = pieces[0].shape[0]
    picker = (wanted[:, None] == jnp.arange(piece_count, dtype=jnp.int32)[None, :]).astype(
        jnp.bfloat16
    )
    left_own = jnp.einsum("js,sxdr->jxdr", picker, pieces[0], preferred_element_type=jnp.float32)
    right_own = jnp.einsum("js,sxrf->jxrf", picker, pieces[1], preferred_element_type=jnp.float32)
    left_narrow = left_own.astype(jnp.bfloat16)
    both_weights = jnp.stack((gate_weight, up_weight), axis=1)
    factor_piece = lax.all_gather(right_own.astype(jnp.bfloat16), "dp", axis=3, tiled=True)
    update = jnp.einsum(
        "jxdr,jxrf->jxdf", left_narrow, factor_piece, preferred_element_type=jnp.float32
    )
    merged = (both_weights.astype(jnp.float32) + update).astype(jnp.bfloat16)
    positions = lax.axis_index("tensor") * span_here + jnp.arange(span_here, dtype=jnp.int32)
    visible = positions[None, :] < lengths[:, None]
    cache_wide = cache.astype(jnp.float32)
    gain_cols = lax.dynamic_slice_in_dim(moe_gain, col_start, part_cols, 0)
    router_rows = lax.dynamic_slice_in_dim(router_weight, col_start, part_cols, 0).astype(
        jnp.float32
    )
    expert_range = jnp.arange(EXPERTS, dtype=jnp.int32)
    slot_range = jnp.arange(EXPERTS * CAP, dtype=jnp.int32)
    fresh_keys = []
    results = []
    for step_index in range(STEPS):
        tokens = inputs[step_index]
        normed = normalized(tokens, attn_gain)
        normed_cols = lax.dynamic_slice_in_dim(normed, col_start, part_cols, 1)
        projected = lax.psum(
            jnp.dot(normed_cols, qkv_weight, preferred_element_type=jnp.float32), "tensor"
        )
        queries = projected[:, :LAT].astype(jnp.bfloat16)
        fresh_keys.append(projected[:, LAT:].astype(jnp.bfloat16))
        cached = (
            jnp.einsum("bl,bpl->bp", queries, cache, preferred_element_type=jnp.float32)
            * score_scale
        )
        local_top = jnp.max(jnp.where(visible, cached, FLOOR), axis=-1)
        cached_weights = jnp.where(visible, jnp.exp(cached - local_top[:, None]), 0.0)
        local_part = (
            local_top,
            jnp.sum(cached_weights, axis=-1),
            jnp.einsum("bp,bpl->bl", cached_weights, cache_wide, precision=lax.Precision.HIGHEST),
        )
        gathered_part = merged_2(local_part, "tensor", softmax_join)
        recent = jnp.stack(fresh_keys, axis=1)
        latest = (
            jnp.einsum("bl,bkl->bk", queries, recent, preferred_element_type=jnp.float32)
            * score_scale
        )
        latest_top = jnp.max(latest, axis=-1)
        latest_weights = jnp.exp(latest - latest_top[:, None])
        own_part = (
            latest_top,
            jnp.sum(latest_weights, axis=-1),
            jnp.einsum(
                "bk,bkl->bl",
                latest_weights,
                recent.astype(jnp.float32),
                precision=lax.Precision.HIGHEST,
            ),
        )
        joined = softmax_join(gathered_part, own_part)
        attended = (joined[2] / joined[1][:, None]).astype(jnp.bfloat16)
        token_cols = lax.dynamic_slice_in_dim(tokens, col_start, part_cols, 1)
        middle = (
            token_cols.astype(jnp.float32)
            + jnp.dot(attended, out_weight, preferred_element_type=jnp.float32)
        ).astype(jnp.bfloat16)
        middle_wide = middle.astype(jnp.float32)
        statistics = lax.psum(
            (
                jnp.sum(middle_wide * middle_wide, axis=-1),
                jnp.dot(middle_wide * gain_cols, router_rows, precision=lax.Precision.HIGHEST),
            ),
            "tensor",
        )
        inverse = lax.rsqrt(statistics[0] / D + EPS)
        routed_in = (middle_wide * inverse[:, None] * gain_cols).astype(jnp.bfloat16)
        logits = inverse[:, None] * statistics[1]
        routes_now = expert_ids[step_index]
        matches = routes_now[:, :, None] == expert_range[None, None, :]
        picked = jnp.sum(jnp.where(matches, logits[:, None, :], 0.0), axis=-1)
        gated_scores = jax.nn.sigmoid(picked)
        route_weights = (
            ROUTE_SCALE * gated_scores / jnp.sum(gated_scores, axis=-1, keepdims=True)
        ).astype(jnp.bfloat16)
        onehot_int = matches.reshape(-1, EXPERTS).astype(jnp.int32)
        earlier = jnp.cumsum(onehot_int, axis=0) - onehot_int
        position = jnp.sum(earlier * onehot_int, axis=1)
        target = routes_now.reshape(-1) * CAP + position
        placing = target.reshape(rows_here, -1)[:, :, None] == slot_range[None, None, :]
        scatter_matrix = jnp.any(placing, axis=1).astype(jnp.bfloat16)
        packed = jnp.einsum(
            "rs,rd->sd", scatter_matrix, routed_in, preferred_element_type=jnp.float32
        ).astype(jnp.bfloat16)
        packed = packed.reshape(shard_count, experts_here, CAP, part_cols)
        preacts = jnp.einsum(
            "sjkd,jxdf->sjkxf",
            lax.all_to_all(packed, "expert", split_axis=0, concat_axis=0, tiled=True),
            merged,
            preferred_element_type=jnp.float32,
        )
        summed = lax.psum(preacts, "tensor")
        hidden = (jax.nn.silu(summed[:, :, :, 0]) * summed[:, :, :, 1]).astype(jnp.bfloat16)
        answered = jnp.einsum(
            "sjkf,jfd->sjkd", hidden, down_weight, preferred_element_type=jnp.float32
        ).astype(jnp.bfloat16)
        returned = lax.all_to_all(
            answered, "expert", split_axis=0, concat_axis=0, tiled=True
        ).reshape(EXPERTS * CAP, part_cols)
        combine_matrix = jnp.sum(
            jnp.where(placing, route_weights[:, :, None], jnp.zeros((), jnp.bfloat16)), axis=1
        )
        mixture = jnp.dot(combine_matrix, returned, preferred_element_type=jnp.float32)
        results.append((middle_wide + mixture).astype(jnp.bfloat16))
    return jnp.stack(results, axis=0)


def solution(mesh):
    return jax.shard_map(
        shards,
        mesh=mesh,
        in_specs=(
            P(None, ("groups", "expert", "dp"), None),
            P(),
            P("tensor", None),
            P(None, "tensor"),
            P(("groups", "expert", "dp"), "tensor", None),
            P(("groups", "expert", "dp")),
            P(),
            P(),
            P(None, ("groups", "expert", "dp"), None),
            P("expert", "tensor", None),
            P("expert", "tensor", None),
            P("expert", None, "tensor"),
            P(("groups", "expert"), None, "tensor", None),
            P(("groups", "expert"), None, None, "dp"),
            P("groups"),
        ),
        out_specs=P(None, ("groups", "expert", "dp"), "tensor"),
        check_vma=False,
    )
```

profile of v0, /device:TPU:0, one launch (start us, length us, event | category | flops | bytes accessed | tf_op | source)
XLA Modules:
  0.0 626.8 jit_solution(1131827410680483413)
XLA Ops:
  6.6 0.7 all-gather.12.cloned.1.call-update
  7.4 0.7 all-gather.10.cloned.1.call-update
  10.2 0.4 fusion.75
  10.5 0.4 fusion.73
  10.9 10.6 %all-reduce.6 = (bf16[16,512]{1,0:T(8,128)(2,1)S(1)}, bf16[16,512]{1,0:T(8,128)(2,1)S(1)}) all-reduce(f32[16,512]{1,0:T(8,128)S(1)} %fusion.75, f32[16,512]{1,0:T(8,128)S(1)} %fusion.73), channel_id=1, replica_groups=mesh['groups'=2,'expert'=4,'tensor'=2,'dp'=2] {'tensor'}, use_global_device_ids=true, to_apply=%region_15.16 | all-reduce | flops 16384 | bytes 98304 | tf_op jit(solution)/shard_map/psum | solution.py:103
  22.0 0.6 dynamic-slice.2
  23.2 0.4 fusion.105
  23.6 0.4 fusion.99
  24.8 0.5 fusion.158
  25.3 0.5 fusion.159
  26.3 4.9 all-reduce.5
  31.2 4.4 all-gather.3
  35.6 4.4 all-gather
  40.5 1.6 multiply_reduce_fusion.2
  42.3 0.4 multiply_reduce_fusion.3
  42.9 6.9 %all-reduce.4 = (f32[16,16]{1,0:T(8,128)S(1)}, f32[16]{0:T(128)S(1)}, f32[16,16]{1,0:T(8,128)S(1)}, f32[16]{0:T(128)S(1)}) all-reduce(f32[16,16]{1,0:T(8,128)S(1)} %fusion.65, f32[16]{0:T(128)S(1)} %get-tuple-element.96, f32[16,16]{1,0:T(8,128)S(1)} %fusion.67, ...), channel_id=1, replica_groups=mesh['groups'=2,'expert'=4,'tensor'=2,'dp'=2] {'tensor'}, use_global_device_ids=true, to_apply=%region_24.25 | all-reduce | flops 544 | bytes 4352 | tf_op jit(solution)/shard_map/psum | solution.py:145
  49.9 0.4 convolution_convert_fusion.1
  50.7 1.4 copy.98
  52.0 5.2 all-to-all-start
  57.6 0.6 gather_fusion
  58.4 52.3 %all-gather.12.cloned.1.call-done = bf16[32,2,64,512]{3,2,1,0:T(8,128)(2,1)} async-done(((bf16[8,2,64,512]{3,2,1,0:T(8,128)(2,1)}), bf16[32,2,64,512]{3,2,1,0:T(8,128)(2,1)}) %all-gather.12.cloned.1.call-update) | async-done | bytes 4194320 | tf_op jit(solution)/shard_map/all_gather | solution.py:73
  110.6 5.4 fusion.42
  116.1 0.4 convolution_convert_fusion
  116.8 1.4 copy.109
  118.2 245.0 %all-gather.10.cloned.1.call-done = bf16[32,2,1792,64]{2,3,1,0:T(8,128)(2,1)} async-done(((bf16[8,2,1792,64]{2,3,1,0:T(8,128)(2,1)}), bf16[32,2,1792,64]{2,3,1,0:T(8,128)(2,1)}) %all-gather.10.cloned.1.call-update) | async-done | bytes 14680080 | tf_op jit(solution)/shard_map/all_gather | solution.py:72
  363.2 21.3 %fusion.12 = bf16[4,2,1792,64]{2,0,3,1:T(4,128)(2,1)S(1)} fusion(bf16[32,2,1792,64]{2,3,1,0:T(8,128)(2,1)} %all-gather.10.cloned.1.call-done, s32[4]{0:T(128)S(1)} %and_select_fusion), kind=kOutput, calls=%fused_computation.14 | convolution fusion | flops 59637888 | bytes 16515088 | tf_op jit(solution)/shard_map/js,sxdr->jxdr/dot_general | solution.py:79
  384.5 21.3 %add_convert_fusion = bf16[4,2,1792,1024]{3,2,1,0:T(8,128)(2,1)} fusion(bf16[4,1,1792,1024]{3,2,1,0:T(8,128)(2,1)} %bitcast.172, bf16[4,1,1792,1024]{3,2,1,0:T(8,128)(2,1)} %bitcast.173, bf16[4,2,1792,64]{2,0,3,1:T(4,128)(2,1)S(1)} %fusion.12, bf16[4,2,64,1024]{3,0,2,1:T(4,128)(2,1)} %all-gather.14.cloned.1.call-done), kind=kOutput, calls=%fused_computation.1 | convolution fusion | flops 1937768448 | bytes 61603840 | tf_op jit(solution)/shard_map/jxdr,jxrf->jxdf/dot_general | solution.py:84
  405.8 3.5 all-to-all-start.2
  409.3 0.3 all-reduce.10.cloned.1.call-start
  409.6 13.4 %fusion.39 = f32[4,4,15,2,1024]{4,2,0,3,1:T(8,128)} fusion(bf16[4,2,1792,1024]{3,2,1,0:T(8,128)(2,1)} %add_convert_fusion, bf16[4,4,15,1792,1]{3,1,2,0,4:T(4,128)(2,1)S(1)} %bitcast.163), kind=kOutput, calls=%fused_computation.35 | convolution fusion | flops 1761607680 | bytes 32186368 | tf_op jit(solution)/shard_map/sjkd,jxdf->sjkxf/dot_general | solution.py:172
  423.0 8.4 %all-to-all-done.2 = bf16[4,4,15,1792]{3,1,2,0:T(4,128)(2,1)S(1)} async-done(((bf16[4,4,15,1792]{3,1,2,0:T(4,128)(2,1)}), bf16[4,4,15,1792]{3,1,2,0:T(4,128)(2,1)S(1)}, u32[]{:S(2)}, u32[]{:S(2)}) %all-to-all-start.2) | async-done | bytes 860192 | tf_op jit(solution)/shard_map/all_to_all | solution.py:174
  431.4 13.4 %fusion.36 = f32[4,4,15,2,1024]{4,2,0,1,3:T(8,128)} fusion(bf16[4,4,15,1792]{3,1,2,0:T(4,128)(2,1)S(1)} %all-to-all-done.2, bf16[4,2,1792,1024]{3,2,1,0:T(8,128)(2,1)} %add_convert_fusion), kind=kOutput, calls=%fused_computation.34 | convolution fusion | flops 1761607680 | bytes 32186368 | tf_op jit(solution)/shard_map/sjkd,jxdf->sjkxf/dot_general | solution.py:172
  445.0 107.3 %all-reduce.10.cloned.1.call-done = (f32[4,4,15,2,1024]{4,2,0,1,3:T(8,128)}, f32[4,4,15,2,1024]{4,2,0,3,1:T(8,128)}) async-done(((f32[4,4,15,2,1024]{4,2,0,1,3:T(8,128)}, f32[4,4,15,2,1024]{4,2,0,3,1:T(8,128)}), (f32[4,4,15,2,1024]{4,2,0,1,3:T(8,128)}, f32[4,4,15,2,1024]{4,2,0,3,1:T(8,128)})) %all-reduce.10.cloned.1.call-update) | async-done | bytes 3932176 | tf_op jit(solution)/shard_map/psum | solution.py:178
  552.2 8.3 %fusion.24 = bf16[4,4,15,1792]{3,2,0,1:T(8,128)(2,1)S(1)} fusion(bf16[4,1024,1792]{2,1,0:T(8,128)(2,1)} %param.26, f32[4,4,15,2,1024]{4,2,0,3,1:T(8,128)} %get-tuple-element.62), kind=kOutput, calls=%fused_computation.20 | convolution fusion | flops 882708480 | bytes 17506304 | tf_op jit(solution)/shard_map/sjkf,jfd->sjkd/dot_general | solution.py:180
  560.5 1.6 copy.101
  562.2 4.6 all-to-all-start.1
  566.8 8.3 %fusion.21 = bf16[4,4,15,1792]{3,2,0,1:T(8,128)(2,1)S(1)} fusion(bf16[4,1024,1792]{2,1,0:T(8,128)(2,1)} %param.26, f32[4,4,15,2,1024]{4,2,0,1,3:T(8,128)} %get-tuple-element.61), kind=kOutput, calls=%fused_computation.19 | convolution fusion | flops 882708480 | bytes 17506304 | tf_op jit(solution)/shard_map/sjkf,jfd->sjkd/dot_general | solution.py:180
  575.1 1.6 copy.112
  576.7 11.8 %all-to-all-done.1 = bf16[4,4,15,1792]{3,1,2,0:T(4,128)(2,1)S(1)} async-done(((bf16[4,4,15,1792]{3,1,2,0:T(4,128)(2,1)}), bf16[4,4,15,1792]{3,1,2,0:T(4,128)(2,1)S(1)}, u32[]{:S(2)}, u32[]{:S(2)}) %all-to-all-start.1) | async-done | bytes 860192 | tf_op jit(solution)/shard_map/all_to_all | solution.py:183
  588.5 4.2 all-to-all-start.3
  593.9 1.4 copy.102
  595.2 1.2 reshape.296
  596.4 17.5 %all-to-all-done.3 = bf16[4,4,15,1792]{3,1,2,0:T(4,128)(2,1)} async-done(((bf16[4,4,15,1792]{3,1,2,0:T(4,128)(2,1)}), bf16[4,4,15,1792]{3,1,2,0:T(4,128)(2,1)}, u32[]{:S(2)}, u32[]{:S(2)}) %all-to-all-start.3) | async-done | bytes 860192 | tf_op jit(solution)/shard_map/all_to_all | solution.py:183
  613.9 1.2 copy.113
  615.2 1.2 reshape.298
  616.4 1.4 fusion.34
  617.7 1.4 fusion.33
  619.2 0.7 pad_maximum_fusion
  (108 shorter events, 6.9 us)
Async XLA Ops:
  6.5 3.6 copy-start
  6.5 1.5 copy-start.9
  6.5 1.6 copy-start.10
  6.5 1.7 copy-start.8
  6.5 3.3 copy-start.6
  6.5 104.1 %all-gather.12.cloned.1.call-start = ((), (), s32[]{:S(2)}) async-start(), calls=%async_computation.5 | async-start | bytes 5242880 | tf_op jit(solution)/shard_map/all_gather | solution.py:73
  7.3 14.7 %copy-start.12 = (u32[32]{0:T(128)S(1)}, u32[32]{0:T(128)}, u32[]{:S(2)}) copy-start(u32[32]{0:T(128)} %constant.94) | copy-start | bytes 388
  7.3 15.9 %copy-start.3 = (bf16[16,128,256]{2,1,0:T(8,128)(2,1)S(1)}, bf16[16,128,256]{2,1,0:T(8,128)(2,1)}, u32[]{:S(2)}) copy-start(bf16[16,128,256]{2,1,0:T(8,128)(2,1)} %param.19) | copy-start | bytes 3145732
  7.3 355.9 %all-gather.10.cloned.1.call-start = ((), (), s32[]{:S(2)}) async-start(), calls=%async_computation.4 | async-start | bytes 18350080 | tf_op jit(solution)/shard_map/all_gather | solution.py:72
  8.1 15.9 %copy-start.11 = (s32[16]{0:T(128)S(1)}, s32[16]{0:T(128)}, u32[]{:S(2)}) copy-start(s32[16]{0:T(128)} %param.20) | copy-start | bytes 196
  10.5 31.6 %copy-start.7 = (bf16[3584,16]{0,1:T(8,128)(2,1)S(1)}, bf16[3584,16]{0,1:T(8,128)(2,1)}, u32[]{:S(2)}) copy-start(bf16[3584,16]{0,1:T(8,128)(2,1)} %param.22) | copy-start | bytes 344068
  10.9 31.4 %copy-start.4 = (bf16[256,1792]{1,0:T(8,128)(2,1)S(1)}, bf16[256,1792]{1,0:T(8,128)(2,1)}, u32[]{:S(2)}) copy-start(bf16[256,1792]{1,0:T(8,128)(2,1)} %param.18) | copy-start | bytes 2752516
  42.1 15.4 %copy-start.2 = (s32[16]{0:T(128)S(1)}, s32[16]{0:T(128)}, u32[]{:S(2)}) copy-start(s32[16]{0:T(128)} %param.29) | copy-start | bytes 196
  52.0 353.7 %all-to-all-start = ((bf16[4,4,15,1792]{3,1,2,0:T(4,128)(2,1)}), bf16[4,4,15,1792]{3,1,2,0:T(4,128)(2,1)S(1)}, u32[]{:S(2)}, u32[]{:S(2)}) async-start(bf16[4,4,15,1792]{3,1,2,0:T(4,128)(2,1)} %copy.98), calls=%async_computation | async-start | bytes 1720320 | tf_op jit(solution)/shard_map/all_to_all | solution.py:174
  57.3 327.2 %all-gather.14.cloned.1.call-start = ((), (), s32[]{:S(2)}) async-start(), calls=%async_computation.6 | async-start | bytes 1572864 | tf_op jit(solution)/shard_map/all_gather | solution.py:83
  405.8 25.7 %all-to-all-start.2 = ((bf16[4,4,15,1792]{3,1,2,0:T(4,128)(2,1)}), bf16[4,4,15,1792]{3,1,2,0:T(4,128)(2,1)S(1)}, u32[]{:S(2)}, u32[]{:S(2)}) async-start(bf16[4,4,15,1792]{3,1,2,0:T(4,128)(2,1)} %copy.109), calls=%async_computation.2 | async-start | bytes 1720320 | tf_op jit(solution)/shard_map/all_to_all | solution.py:174
  409.3 142.9 %all-reduce.10.cloned.1.call-start = ((), (), s32[]{:S(2)}) async-start(), calls=%async_computation.7 | async-start | bytes 8388608 | tf_op jit(solution)/shard_map/psum | solution.py:178
  562.2 26.3 %all-to-all-start.1 = ((bf16[4,4,15,1792]{3,1,2,0:T(4,128)(2,1)}), bf16[4,4,15,1792]{3,1,2,0:T(4,128)(2,1)S(1)}, u32[]{:S(2)}, u32[]{:S(2)}) async-start(bf16[4,4,15,1792]{3,1,2,0:T(4,128)(2,1)} %copy.101), calls=%async_computation.1 | async-start | bytes 1720320 | tf_op jit(solution)/shard_map/all_to_all | solution.py:183
  588.5 5.2 copy-start.5
  588.5 25.5 %all-to-all-start.3 = ((bf16[4,4,15,1792]{3,1,2,0:T(4,128)(2,1)}), bf16[4,4,15,1792]{3,1,2,0:T(4,128)(2,1)}, u32[]{:S(2)}, u32[]{:S(2)}) async-start(bf16[4,4,15,1792]{3,1,2,0:T(4,128)(2,1)} %copy.112), calls=%async_computation.3 | async-start | bytes 1720320 | tf_op jit(solution)/shard_map/all_to_all | solution.py:183
  593.8 26.0 %copy-start.1 = (bf16[1792,512]{1,0:T(8,128)(2,1)S(1)}, bf16[1792,512]{1,0:T(8,128)(2,1)}, u32[]{:S(2)}) copy-start(bf16[1792,512]{1,0:T(8,128)(2,1)} %param.17) | copy-start | bytes 5505028
Sparse Core Ops, SparseCore 0:
  9.0 101.6 all-gather.11
  112.2 250.9 all-gather.9
  364.7 7.1 all-gather.13
  445.0 107.2 all-reduce.9
where the time goes:
time: 632 us; the launch traced here: 627 us
  waiting for transfers between devices  444 us (70%)
  matrix products  100 us (16%)
  blocking collectives  31.2 us (5%)
  starting transfers between devices  18.1 us (3%)
  local copies, waits for them, and re-layouts  15.3 us (2%)
  between operations  14.7 us (2%)
    all_gather x1, waiting for transfers between devices, shards(): lax.all_gather(pool_left, 'expert', axis=0, tiled=True)  245 us
    psum x1, waiting for transfers between devices, shards(): summed = lax.psum(preacts, 'tensor')  107 us
    all_gather x1, waiting for transfers between devices, shards(): lax.all_gather(pool_right, 'expert', axis=0, tiled=True)  52.3 us
    all_to_all x2, waiting for transfers between devices, shards(): lax.all_to_all(answered, 'expert', split_axis=0, concat_axis=0, tiled=True)  29.2 us
    dot_general x2, matrix products, shards(): jnp.einsum('sjkd,jxdf->sjkxf', lax.all_to_all(packed, 'expert', split_axi...  26.8 us
    dot_general x1, matrix products, shards(): jnp.einsum('jxdr,jxrf->jxdf', left_narrow, factor_piece, preferred_elemen...  21.3 us
    dot_general x1, matrix products, shards(): jnp.einsum('js,sxdr->jxdr', picker, pieces[0], preferred_element_type=jnp...  21.3 us
    dot_general x2, matrix products, shards(): jnp.einsum('sjkf,jfd->sjkd', hidden, down_weight, preferred_element_type=...  16.6 us
  transfers between devices with their start and end apart: 8, of which 6 were waited for; matrix products, arithmetic and copies ran while one was open for 14% of the time, Pallas kernels for 0%

commit v1 on v0

v1 whole, which is shorter than its diff:
```python
import jax
import jax.numpy as jnp
from jax import lax
from jax.sharding import PartitionSpec as P

EPS = 1e-06
ROUTE_SCALE = 2.5
FLOOR = -1e30
F32 = jnp.float32
BF16 = jnp.bfloat16


def split_terms(value, count):
    terms = []
    for _ in range(count):
        term = lax.reduce_precision(value, 8, 7)
        terms.append(term.astype(BF16))
        value = value - term
    return terms


def shards(
    inputs,
    attn_gain,
    qkv_weight,
    out_weight,
    cache,
    lengths,
    moe_gain,
    router_weight,
    expert_ids,
    gate_weight,
    up_weight,
    down_weight,
    pool_left,
    pool_right,
    pair_slot,
):
    steps, rows_here, width = inputs.shape
    experts_here, part_cols, ffw = gate_weight.shape
    slots_here, _, _, rank = pool_left.shape
    right_cols = pool_right.shape[3]
    lat = cache.shape[2]
    span_here = cache.shape[1]
    shard_count = lax.axis_size("expert")
    shard_index = lax.axis_index("expert")
    tensor_count = lax.axis_size("tensor")
    tensor_index = lax.axis_index("tensor")
    expert_count = shard_count * experts_here
    col_start = tensor_index * part_cols
    batch = steps * rows_here
    total_rows = shard_count * batch
    score_scale = lat ** (-0.5)
    paired = tensor_count == 2

    own_slots = shard_index * slots_here + jnp.arange(slots_here, dtype=jnp.int32)
    serves = (pair_slot[:, None] == own_slots[None, :]).astype(BF16)

    piece_cols = right_cols // tensor_count
    right_piece = lax.dynamic_slice_in_dim(pool_right, tensor_index * piece_cols, piece_cols, 3)
    right_sent = jnp.einsum(
        "es,sxrf->exrf", serves, right_piece, preferred_element_type=F32
    ).astype(BF16)
    right_sent = right_sent.reshape(shard_count, experts_here, 2, rank, piece_cols)
    right_got = lax.all_to_all(right_sent, "expert", split_axis=0, concat_axis=0, tiled=True)
    right_own = jnp.sum(right_got.astype(F32), axis=0).astype(BF16)
    right_full = lax.all_gather(right_own, ("dp", "tensor"), axis=3, tiled=True)

    chosen = jnp.any(
        expert_ids.reshape(batch, -1)[:, :, None]
        == jnp.arange(expert_count, dtype=jnp.int32)[None, None, :],
        axis=1,
    ).astype(BF16)
    chosen_all = lax.all_gather(chosen, "expert", axis=0, tiled=False)

    tokens = inputs.reshape(batch, width)
    tokens_wide = tokens.astype(F32)
    square_mean = jnp.mean(tokens_wide * tokens_wide, axis=-1, keepdims=True)
    token_cols = lax.dynamic_slice_in_dim(tokens, col_start, part_cols, 1)
    gain_piece = lax.dynamic_slice_in_dim(attn_gain, col_start, part_cols, 0)
    normed_cols = (
        token_cols.astype(F32) * lax.rsqrt(square_mean + EPS) * gain_piece
    ).astype(BF16)
    projected = lax.psum(jnp.dot(normed_cols, qkv_weight, preferred_element_type=F32), "tensor")
    queries = projected[:, :lat].astype(BF16).reshape(steps, rows_here, lat)
    fresh = projected[:, lat:].astype(BF16).reshape(steps, rows_here, lat)

    positions = tensor_index * span_here + jnp.arange(span_here, dtype=jnp.int32)
    visible = (positions[None, :] < lengths[:, None])[:, None, :]
    scores = (
        jnp.einsum("sbl,bpl->bsp", queries, cache, preferred_element_type=F32) * score_scale
    )
    local_top = jnp.max(jnp.where(visible, scores, FLOOR), axis=-1, keepdims=True)
    weights = jnp.where(visible, jnp.exp(scores - local_top), 0.0)
    terms = jnp.concatenate(split_terms(weights, 3), axis=1)
    sums = jnp.einsum("bmp,bpl->bml", terms, cache, preferred_element_type=F32)
    sums = jnp.sum(sums.reshape(rows_here, 3, steps, lat), axis=1)
    local_total = jnp.sum(weights, axis=-1, keepdims=True)
    packed = jnp.concatenate(
        (
            sums,
            jnp.broadcast_to(local_top, (rows_here, steps, 64)),
            jnp.broadcast_to(local_total, (rows_here, steps, 64)),
        ),
        axis=2,
    )
    parts = lax.all_gather(packed, "tensor", axis=0, tiled=False)
    part_sums, part_tops, part_totals = (
        parts[..., :lat],
        parts[..., lat],
        parts[..., lat + 64],
    )

    fresh_wide = fresh.astype(F32)
    latest = (
        jnp.sum(queries.astype(F32)[:, None] * fresh_wide[None], axis=-1) * score_scale
    )
    step_range = jnp.arange(steps)
    usable = (step_range[None, :] <= step_range[:, None])[:, :, None]
    latest_top = jnp.max(jnp.where(usable, latest, FLOOR), axis=1)
    highest = jnp.maximum(jnp.max(part_tops, axis=0), latest_top.T)
    factors = jnp.exp(part_tops - highest[None])
    latest_weights = jnp.where(usable, jnp.exp(latest - highest.T[:, None, :]), 0.0)
    denominator = jnp.sum(part_totals * factors, axis=0) + jnp.sum(latest_weights, axis=1).T
    numerator = jnp.sum(part_sums * factors[..., None], axis=0).transpose(1, 0, 2) + jnp.sum(
        latest_weights[..., None] * fresh_wide[None], axis=1
    )
    attended = (numerator / denominator.T[..., None]).astype(BF16).reshape(batch, lat)
    middle = (
        token_cols.astype(F32) + jnp.dot(attended, out_weight, preferred_element_type=F32)
    ).astype(BF16)

    gain_cols = lax.dynamic_slice_in_dim(moe_gain, col_start, part_cols, 0)
    router_rows = lax.dynamic_slice_in_dim(router_weight, col_start, part_cols, 0).astype(F32)
    middle_wide = middle.astype(F32)
    partial_logits = jnp.dot(
        middle_wide * gain_cols, router_rows, precision=lax.Precision.HIGHEST
    )
    partial_squares = jnp.sum(middle_wide * middle_wide, axis=-1, keepdims=True)
    statistics = jnp.concatenate(
        (partial_logits, jnp.broadcast_to(partial_squares, (batch, 128 - expert_count))), axis=1
    )
    statistics = lax.all_gather(statistics, ("expert", "tensor"), axis=0, tiled=False)
    statistics = jnp.sum(
        statistics.reshape(shard_count, tensor_count, batch, 128), axis=1
    )
    middle_all = lax.all_gather(middle, "expert", axis=0, tiled=False)

    def turned(value):
        if not paired:
            return value
        half = shard_count // 2
        swapped = jnp.concatenate((value[half:], value[:half]), axis=0)
        return jnp.where(tensor_index == 0, value, swapped)

    statistics = turned(statistics).reshape(total_rows, 128)
    rows_all = turned(middle_all).reshape(total_rows, part_cols)
    mask_all = turned(chosen_all).reshape(total_rows, expert_count).astype(F32)

    inverse = lax.rsqrt(statistics[:, 127:] / width + EPS)
    routed_in = (rows_all.astype(F32) * inverse * gain_cols).astype(BF16)
    gated = jax.nn.sigmoid(inverse * statistics[:, :expert_count]) * mask_all
    route = (ROUTE_SCALE * gated / jnp.sum(gated, axis=-1, keepdims=True)).astype(BF16)
    route_here = lax.dynamic_slice_in_dim(
        route, shard_index * experts_here, experts_here, 1
    ).astype(F32)

    low = jnp.einsum("nd,sxdr->sxnr", routed_in, pool_left, preferred_element_type=F32)
    low_sent = jnp.einsum(
        "es,sxnr->exnr", serves, low.astype(BF16), preferred_element_type=F32
    ).astype(BF16)
    low_sent = low_sent.reshape(shard_count, experts_here, 2, total_rows, rank)
    low_got = lax.all_to_all(low_sent, "expert", split_axis=0, concat_axis=0, tiled=True)
    low_own = jnp.sum(low_got.astype(F32), axis=0).astype(BF16)

    exchange = [(0, 1), (1, 0)]
    mixture = jnp.zeros((total_rows, part_cols), F32)
    for expert in range(experts_here):
        partial = [
            jnp.dot(routed_in, weight[expert], preferred_element_type=F32)
            + jnp.dot(
                low_own[expert, which], right_full[expert, which], preferred_element_type=F32
            )
            for which, weight in enumerate((gate_weight, up_weight))
        ]
        if paired:
            half_rows = total_rows // 2
            sent = jnp.concatenate([value[half_rows:].astype(BF16) for value in partial], axis=1)
            got = lax.ppermute(sent, "tensor", exchange).astype(F32)
            gate = partial[0][:half_rows] + got[:, :ffw]
            up = partial[1][:half_rows] + got[:, ffw:]
            hidden = (jax.nn.silu(gate) * up).astype(BF16)
            hidden = jnp.concatenate(
                (hidden, lax.ppermute(hidden, "tensor", exchange)), axis=0
            )
        else:
            summed = lax.psum_scatter(
                jnp.concatenate(partial, axis=1), "tensor", scatter_dimension=0, tiled=True
            )
            hidden = (jax.nn.silu(summed[:, :ffw]) * summed[:, ffw:]).astype(BF16)
            hidden = lax.all_gather(hidden, "tensor", axis=0, tiled=True)
        answered = jnp.dot(hidden, down_weight[expert], preferred_element_type=F32).astype(BF16)
        mixture = mixture + route_here[:, expert : expert + 1] * answered.astype(F32)

    returned = turned(mixture.astype(BF16).reshape(shard_count, batch, part_cols))
    returned = lax.all_to_all(returned, "expert", split_axis=0, concat_axis=0, tiled=True)
    outputs = (middle_wide + jnp.sum(returned.astype(F32), axis=0)).astype(BF16)
    return outputs.reshape(steps, rows_here, part_cols)


def solution(mesh):
    return jax.shard_map(
        shards,
        mesh=mesh,
        in_specs=(
            P(None, ("groups", "expert", "dp"), None),
            P(),
            P("tensor", None),
            P(None, "tensor"),
            P(("groups", "expert", "dp"), "tensor", None),
            P(("groups", "expert", "dp")),
            P(),
            P(),
            P(None, ("groups", "expert", "dp"), None),
            P("expert", "tensor", None),
            P("expert", "tensor", None),
            P("expert", None, "tensor"),
            P(("groups", "expert"), None, "tensor", None),
            P(("groups", "expert"), None, None, "dp"),
            P("groups"),
        ),
        out_specs=P(None, ("groups", "expert", "dp"), "tensor"),
        check_vma=False,
    )
```

time: 632 us -> 215 us (0.34)
  waiting for transfers between devices: 444 us -> 32.6 us
  matrix products: 100 us -> 38.1 us
  blocking collectives: 31.2 us -> 91.9 us
    all_gather x3 -> x1, waiting for transfers between devices: 297 us -> 7.81 us  [shards(): right_full = lax.all_gather(right_own, ('dp', 'tensor'), axis=3, tiled=True)]
    psum x1 -> x0, waiting for transfers between devices: 107 us -> none  [shards(): summed = lax.psum(preacts, 'tensor')]
    dot_general x21 -> x26, matrix products: 100 us -> 37.9 us  [the longest x8 24.2 us: shards(): jnp.dot(routed_in, weight[expert], preferred_element_type=F32)]
    all_gather x2 -> x4, blocking collectives: 8.81 us -> 66.4 us  [the longest x1 30.5 us: shards(): lax.all_gather(statistics, ('expert', 'tensor'), axis=0, tiled=False)]
    all_to_all x4 -> x2, waiting for transfers between devices: 37.7 us -> 0.01 us  [the longest x1 0.01 us: shards(): lax.all_to_all(low_sent, 'expert', split_axis=0, concat_axis=0, tiled=True)]
    ppermute x0 -> x8, waiting for transfers between devices: none -> 24.8 us  [the longest x4 18.8 us: shards(): got = lax.ppermute(sent, 'tensor', exchange).astype(F32)]
    all_to_all x0 -> x1, blocking collectives: none -> 16.5 us  [shards(): lax.all_to_all(returned, 'expert', split_axis=0, concat_axis=0, tiled=True)]
    psum x2 -> x1, blocking collectives: 17.5 us -> 9 us  [shards(): lax.psum(jnp.dot(normed_cols, qkv_weight, preferred_element_type=F32), 't...]
  transfers between devices with their start and end apart: 8 -> 11, of which waited for: 6 -> 5; matrix products, arithmetic and copies ran while one was open for 14% -> 21% of each run, Pallas kernels for 0% -> 0%
where the time goes in v1:
time: 215 us; the launch traced here: 214 us
  blocking collectives  91.9 us (43%)
  matrix products  38.1 us (18%)
  waiting for transfers between devices  32.6 us (15%)
  starting transfers between devices  17.3 us (8%)
  between operations  14.3 us (7%)
  local copies, waits for them, and re-layouts  13.5 us (6%)
  other arithmetic  6.29 us (3%)
    all_gather x1, blocking collectives, shards(): lax.all_gather(statistics, ('expert', 'tensor'), axis=0, tiled=False)  30.5 us
    dot_general x8, matrix products, shards(): jnp.dot(routed_in, weight[expert], preferred_element_type=F32)  24.2 us
    ppermute x4, waiting for transfers between devices, shards(): got = lax.ppermute(sent, 'tensor', exchange).astype(F32)  18.8 us
    all_gather x1, blocking collectives, shards(): middle_all = lax.all_gather(middle, 'expert', axis=0, tiled=False)  18 us
    all_to_all x1, blocking collectives, shards(): lax.all_to_all(returned, 'expert', split_axis=0, concat_axis=0, tiled=True)  16.5 us
    all_gather x1, blocking collectives, shards(): chosen_all = lax.all_gather(chosen, 'expert', axis=0, tiled=False)  13.1 us
    psum x1, blocking collectives, shards(): lax.psum(jnp.dot(normed_cols, qkv_weight, preferred_element_type=F32), 't...  9 us
    all_gather x1, waiting for transfers between devices, shards(): right_full = lax.all_gather(right_own, ('dp', 'tensor'), axis=3, tiled=True)  7.81 us
  transfers between devices with their start and end apart: 11, of which 5 were waited for; matrix products, arithmetic and copies ran while one was open for 21% of the time, Pallas kernels for 0%

profile of v1, /device:TPU:0, one launch (start us, length us, event | category | flops | bytes accessed | tf_op | source)
XLA Modules:
  0.0 213.9 jit_solution(7764491989092929861)
XLA Ops:
  6.5 1.2 constant_dynamic-slice_fusion
  7.8 1.3 convolution_convert_fusion
  9.1 1.1 reshape.226
  10.2 2.7 %copy.114 = bf16[4,4,2,64,256]{4,1,3,2,0:T(4,128)(2,1)} copy(bf16[4,4,2,64,256]{4,1,0,3,2:T(4,128)(2,1)} %reshape.226) | data formatting | bytes 2097152 | tf_op jit(solution)/shard_map/reshape | solution.py:64
  12.9 6.3 %all-to-all-start.1 = ((bf16[4,4,2,64,256]{4,1,3,2,0:T(4,128)(2,1)}), bf16[4,4,2,64,256]{4,1,3,2,0:T(4,128)(2,1)}, u32[]{:S(2)}, u32[]{:S(2)}) async-start(bf16[4,4,2,64,256]{4,1,3,2,0:T(4,128)(2,1)} %copy.114), calls=%async_computation.1 | async-start | bytes 2097152 | tf_op jit(solution)/shard_map/all_to_all | solution.py:65
  19.5 0.5 fusion.142
  20.0 9.0 %psum.7 = bf16[32,512]{1,0:T(8,128)(2,1)S(1)} all-reduce(f32[32,512]{1,0:T(8,128)S(1)} %fusion.142), channel_id=1, replica_groups=mesh['groups'=2,'expert'=4,'tensor'=2,'dp'=2] {'tensor'}, use_global_device_ids=true, to_apply=%region_1.0 | all-reduce | flops 16384 | bytes 98304 | tf_op jit(solution)/shard_map/psum | solution.py:84
  29.1 0.4 fusion.177
  30.3 4.8 %all-gather = f32[32,2,384]{2,0,1:T(8,128)S(1)} all-gather(f32[16,2,384]{2,0,1:T(8,128)S(1)} %pad_maximum_fusion.4), channel_id=2, replica_groups=mesh['groups'=2,'expert'=4,'tensor'=2,'dp'=2] {'tensor'}, dimensions={0}, use_global_device_ids=true | all-gather | bytes 147456 | tf_op jit(solution)/shard_map/all_gather | solution.py:107
  36.0 0.4 fusion.124
  36.4 18.0 %all-gather.3 = bf16[128,1792]{1,0:T(8,128)(2,1)S(1)} all-gather(bf16[32,1792]{1,0:T(8,128)(2,1)S(1)} %get-tuple-element.50), channel_id=5, replica_groups=mesh['groups'=2,'expert'=4,'tensor'=2,'dp'=2] {'expert'}, dimensions={0}, use_global_device_ids=true | all-gather | bytes 573440 | tf_op jit(solution)/shard_map/all_gather | solution.py:147
  54.9 30.5 %all-gather.1 = f32[256,128]{1,0:T(8,128)S(1)} all-gather(f32[32,128]{1,0:T(8,128)S(1)} %pad_maximum_fusion.6), channel_id=3, replica_groups=mesh['groups'=2,'expert'=4,'tensor'=2,'dp'=2] {'expert','tensor'}, dimensions={0}, use_global_device_ids=true | all-gather | bytes 147456 | tf_op jit(solution)/shard_map/all_gather | solution.py:143
  86.1 4.3 %convolution_convert_fusion.1 = bf16[16,2,128,64]{2,0,3,1:T(8,128)(2,1)S(1)} fusion(bf16[8,2,1792,64]{2,3,1,0:T(8,128)(2,1)} %param.27, bf16[128,1792]{1,0:T(8,128)(2,1)S(1)} %fusion.96, s32[16]{0:T(128)S(1)} %copy-done.22, s32[8]{0:T(128)S(1)} %iota_add_fusion), kind=kOutput, calls=%fused_computation.57 | convolution fusion | flops 474349696 | bytes 4653152 | tf_op jit(solution)/shard_map/es,sxnr->exnr/dot_general | solution.py:169
  90.5 1.0 copy.111
  91.7 13.1 %all-gather.4 = bf16[4,32,16]{1,2,0:T(8,128)(2,1)S(1)} all-gather(bf16[1,32,16]{1,2,0:T(8,128)(2,1)S(1)} %convert_bitcast_fusion), channel_id=4, replica_groups=mesh['groups'=2,'expert'=4,'tensor'=2,'dp'=2] {'expert'}, dimensions={0}, use_global_device_ids=true | all-gather | bytes 5120 | tf_op jit(solution)/shard_map/all_gather | solution.py:74
  104.9 2.7 %fusion.2 = f32[128,1024]{1,0:T(8,128)S(1)} fusion(bf16[128,1792]{1,0:T(8,128)(2,1)S(1)} %bitcast.229, bf16[4,1792,1024]{2,1,0:T(8,128)(2,1)} %param.25), kind=kOutput, calls=%fused_computation.2 | convolution fusion | flops 469762048 | bytes 4653056 | tf_op jit(solution)/shard_map/dot_general | solution.py:180
  107.6 3.5 %fusion.8 = f32[128,1024]{1,0:T(8,128)} fusion(bf16[128,1792]{1,0:T(8,128)(2,1)S(1)} %bitcast.230, bf16[4,1792,1024]{2,1,0:T(8,128)(2,1)} %param.25), kind=kOutput, calls=%fused_computation.8 | convolution fusion | flops 469762048 | bytes 4653056 | tf_op jit(solution)/shard_map/dot_general | solution.py:180
  111.1 3.5 %fusion.4 = f32[128,1024]{1,0:T(8,128)} fusion(bf16[128,1792]{1,0:T(8,128)(2,1)S(1)} %bitcast.231, bf16[4,1792,1024]{2,1,0:T(8,128)(2,1)} %param.24), kind=kOutput, calls=%fused_computation.4 | convolution fusion | flops 469762048 | bytes 4653056 | tf_op jit(solution)/shard_map/dot_general | solution.py:180
  114.6 2.7 %fusion.10 = f32[128,1024]{1,0:T(8,128)S(1)} fusion(bf16[128,1792]{1,0:T(8,128)(2,1)S(1)} %bitcast.232, bf16[4,1792,1024]{2,1,0:T(8,128)(2,1)} %param.24), kind=kOutput, calls=%fused_computation.10 | convolution fusion | flops 469762048 | bytes 4653056 | tf_op jit(solution)/shard_map/dot_general | solution.py:180
  117.3 2.7 %fusion.22 = f32[128,1024]{1,0:T(8,128)S(1)} fusion(bf16[128,1792]{1,0:T(8,128)(2,1)S(1)} %bitcast.233, bf16[4,1792,1024]{2,1,0:T(8,128)(2,1)} %param.24), kind=kOutput, calls=%fused_computation.22 | convolution fusion | flops 469762048 | bytes 4653056 | tf_op jit(solution)/shard_map/dot_general | solution.py:180
  120.0 3.5 %all-to-all-start = ((bf16[4,4,2,128,64]{3,1,4,2,0:T(4,128)(2,1)}), bf16[4,4,2,128,64]{3,1,4,2,0:T(4,128)(2,1)S(1)}, u32[]{:S(2)}, u32[]{:S(2)}) async-start(bf16[4,4,2,128,64]{3,1,4,2,0:T(4,128)(2,1)} %copy.111), calls=%async_computation | async-start | bytes 1048576 | tf_op jit(solution)/shard_map/all_to_all | solution.py:173
  123.7 2.5 %reduce_sum.147 = bf16[4,2,64,256]{3,0,2,1:T(4,128)(2,1)} reduce(bf16[4,4,2,64,256]{4,1,3,2,0:T(4,128)(2,1)} %all-to-all-done.1, bf16[]{:T(256)} %constant.55.clone.1), dimensions={0}, to_apply=%region_17.18 | reduce | flops 393216 | bytes 1310722 | tf_op jit(solution)/shard_map/reduce_sum | solution.py:66
  126.3 2.8 %fusion.20 = f32[128,1024]{1,0:T(8,128)S(1)} fusion(bf16[128,1792]{1,0:T(8,128)(2,1)} %bitcast.234, bf16[4,1792,1024]{2,1,0:T(8,128)(2,1)} %param.25), kind=kOutput, calls=%fused_computation.20 | convolution fusion | flops 469762048 | bytes 4653056 | tf_op jit(solution)/shard_map/dot_general | solution.py:180
  129.2 0.6 slice_bitcast_fusion
  129.8 3.5 %fusion.16 = f32[128,1024]{1,0:T(8,128)} fusion(bf16[128,1792]{1,0:T(8,128)(2,1)S(1)} %bitcast.235, bf16[4,1792,1024]{2,1,0:T(8,128)(2,1)} %param.24), kind=kOutput, calls=%fused_computation.16 | convolution fusion | flops 469762048 | bytes 4653056 | tf_op jit(solution)/shard_map/dot_general | solution.py:180
  133.3 2.8 %fusion.14 = f32[128,1024]{1,0:T(8,128)S(1)} fusion(bf16[128,1792]{1,0:T(8,128)(2,1)S(1)} %bitcast.236, bf16[4,1792,1024]{2,1,0:T(8,128)(2,1)} %param.25), kind=kOutput, calls=%fused_computation.14 | convolution fusion | flops 469762048 | bytes 4653056 | tf_op jit(solution)/shard_map/dot_general | solution.py:180
  136.1 0.3 reduce_sum.146
  136.4 0.9 fusion.206
  137.3 7.8 %all-gather.7.cloned.1.call-done = bf16[4,2,64,1024]{3,0,2,1:T(4,128)(2,1)} async-done(((bf16[4,2,64,256]{3,0,2,1:T(4,128)(2,1)}), bf16[4,2,64,1024]{3,0,2,1:T(4,128)(2,1)}) %all-gather.7.cloned.1.call-update) | async-done | bytes 1048592 | tf_op jit(solution)/shard_map/all_gather | solution.py:67
  145.1 4.6 %fusion.203 = (bf16[1,1,64,1024]{3,0,2,1:T(2,128)(2,1)S(1)}, bf16[1,1,64,1024]{3,0,2,1:T(2,128)(2,1)S(1)}, bf16[1,1,64,1024]{3,0,2,1:T(2,128)(2,1)S(1)}, bf16[1,...) fusion(bf16[4,2,64,1024]{3,0,2,1:T(4,128)(2,1)} %all-gather.7.c, ...), kind=kLoop, calls=%fused_computation.244 | loop fusion | bytes 2097152 | tf_op jit(solution)/shard_map/slice | solution.py:182
  150.4 0.4 collective-permute-start.6
  151.4 1.8 collective-permute-start.4
  153.7 0.4 collective-permute-start
  154.7 1.8 collective-permute-start.2
  156.5 3.1 %collective-permute-done.6 = bf16[64,2048]{1,0:T(8,128)(2,1)S(1)} collective-permute-done((bf16[64,2048]{1,0:T(8,128)(2,1)S(1)}, bf16[64,2048]{1,0:T(8,128)(2,1)S(1)}, u32[]{:S(2)}, u32[]{:S(2)}) %collective-permute-start.6) | collective-permute-done | bytes 262176 | tf_op jit(solution)/shard_map/ppermute | solution.py:189
  159.7 0.4 collective-permute-start.7
  160.1 5.1 %collective-permute-done.4 = bf16[64,2048]{1,0:T(8,128)(2,1)S(1)} collective-permute-done((bf16[64,2048]{1,0:T(8,128)(2,1)S(1)}, bf16[64,2048]{1,0:T(8,128)(2,1)S(1)}, u32[]{:S(2)}, u32[]{:S(2)}) %collective-permute-start.4) | collective-permute-done | bytes 262176 | tf_op jit(solution)/shard_map/ppermute | solution.py:189
  165.4 0.4 collective-permute-start.5
  165.7 10.7 %collective-permute-done.2 = bf16[64,2048]{1,0:T(8,128)(2,1)S(1)} collective-permute-done((bf16[64,2048]{1,0:T(8,128)(2,1)S(1)}, bf16[64,2048]{1,0:T(8,128)(2,1)S(1)}, u32[]{:S(2)}, u32[]{:S(2)}) %collective-permute-start.2) | collective-permute-done | bytes 262176 | tf_op jit(solution)/shard_map/ppermute | solution.py:189
  176.6 0.4 collective-permute-start.3
  177.2 1.8 collective-permute-start.1
  178.9 5.9 %collective-permute-done.3 = bf16[64,1024]{1,0:T(8,128)(2,1)S(1)} collective-permute-done((bf16[64,1024]{1,0:T(8,128)(2,1)S(1)}, bf16[64,1024]{1,0:T(8,128)(2,1)S(1)}, u32[]{:S(2)}, u32[]{:S(2)}) %collective-permute-start.3) | collective-permute-done | bytes 131104 | tf_op jit(solution)/shard_map/ppermute | solution.py:194
  184.9 2.7 %fusion.74 = f32[128,1792]{1,0:T(8,128)S(1)} fusion(bf16[4,1024,1792]{2,1,0:T(8,128)(2,1)} %param.26, f32[128]{0:T(128)S(1)} %copy-done.27, bf16[64,1024]{1,0:T(8,128)(2,1)S(1)} %collective-permute-done.3, bf16[64,1024]{1,0:T(8,128)(2,1)S(1)} %fusion.106), kind=kOutput, calls=%fused_computation.50 | convolution fusion | flops 470974464 | bytes 4850176 | tf_op jit(solution)/shard_map/dot_general | solution.py:202
  187.6 0.7 fusion.83
  188.3 0.7 fusion.68
  189.1 0.7 fusion.59
  189.9 16.5 %all_to_all.15 = bf16[4,32,1792]{2,1,0:T(8,128)(2,1)S(1)} all-to-all(bf16[4,32,1792]{2,1,0:T(8,128)(2,1)S(1)} %maximum_select_fusion.1), channel_id=1, replica_groups=mesh['groups'=2,'expert'=4,'tensor'=2,'dp'=2] {'expert'}, dimensions={0} | all-to-all | bytes 917504 | tf_op jit(solution)/shard_map/all_to_all | solution.py:206
  206.4 0.7 fusion.125
  (161 shorter events, 6.9 us)
Async XLA Ops:
  6.5 13.0 %copy-start = (bf16[1792,512]{1,0:T(8,128)(2,1)S(1)}, bf16[1792,512]{1,0:T(8,128)(2,1)}, u32[]{:S(2)}) copy-start(bf16[1792,512]{1,0:T(8,128)(2,1)} %param.17) | copy-start | bytes 5505028
  7.8 11.4 %copy-start.4 = (bf16[2,16,3584]{2,1,0:T(8,128)(2,1)S(1)}, bf16[2,16,3584]{2,1,0:T(8,128)(2,1)}, u32[]{:S(2)}) copy-start(bf16[2,16,3584]{2,1,0:T(8,128)(2,1)} %param.15) | copy-start | bytes 688132
  7.8 11.7 %copy-start.20 = (f32[3584]{0:T(1024)S(1)}, f32[3584]{0:T(1024)}, u32[]{:S(2)}) copy-start(f32[3584]{0:T(1024)} %param.16) | copy-start | bytes 43012
  10.2 18.9 %copy-start.2 = (bf16[16,128,256]{2,1,0:T(8,128)(2,1)S(1)}, bf16[16,128,256]{2,1,0:T(8,128)(2,1)}, u32[]{:S(2)}) copy-start(bf16[16,128,256]{2,1,0:T(8,128)(2,1)} %param.19) | copy-start | bytes 3145732
  10.2 19.3 %copy-start.23 = (s32[16]{0:T(128)S(1)}, s32[16]{0:T(128)}, u32[]{:S(2)}) copy-start(s32[16]{0:T(128)} %param.20) | copy-start | bytes 196
  12.9 107.1 %all-to-all-start.1 = ((bf16[4,4,2,64,256]{4,1,3,2,0:T(4,128)(2,1)}), bf16[4,4,2,64,256]{4,1,3,2,0:T(4,128)(2,1)}, u32[]{:S(2)}, u32[]{:S(2)}) async-start(bf16[4,4,2,64,256]{4,1,3,2,0:T(4,128)(2,1)} %copy.114), calls=%async_computation.1 | async-start | bytes 2097152 | tf_op jit(solution)/shard_map/all_to_all | solution.py:65
  20.0 16.0 %copy-start.3 = (bf16[256,1792]{1,0:T(8,128)(2,1)S(1)}, bf16[256,1792]{1,0:T(8,128)(2,1)}, u32[]{:S(2)}) copy-start(bf16[256,1792]{1,0:T(8,128)(2,1)} %param.18) | copy-start | bytes 2752516
  20.0 34.5 %copy-start.21 = (f32[3584]{0:T(1024)S(1)}, f32[3584]{0:T(1024)}, u32[]{:S(2)}) copy-start(f32[3584]{0:T(1024)} %param.21) | copy-start | bytes 43012
  20.0 34.5 %copy-start.18 = (bf16[3584,16]{0,1:T(8,128)(2,1)S(1)}, bf16[3584,16]{0,1:T(8,128)(2,1)}, u32[]{:S(2)}) copy-start(bf16[3584,16]{0,1:T(8,128)(2,1)} %param.22) | copy-start | bytes 344068
  36.0 50.2 %copy-start.22 = (s32[16]{0:T(128)S(1)}, s32[16]{0:T(128)}, u32[]{:S(2)}) copy-start(s32[16]{0:T(128)} %param.29) | copy-start | bytes 196
  86.0 31.3 %copy-start.8 = (bf16[4,32,1792]{2,1,0:T(8,128)(2,1)}, bf16[4,32,1792]{2,1,0:T(8,128)(2,1)S(1)}, u32[]{:S(2)}) copy-start(bf16[4,32,1792]{2,1,0:T(8,128)(2,1)S(1)} %get-tuple-element.5) | copy-start | bytes 1376260
  86.0 5.5 %copy-start.19 = (s32[2,16,8]{1,2,0:T(8,128)S(1)}, s32[2,16,8]{1,2,0:T(8,128)}, u32[]{:S(2)}) copy-start(s32[2,16,8]{1,2,0:T(8,128)} %param.23) | copy-start | bytes 3076
  120.0 16.1 %all-to-all-start = ((bf16[4,4,2,128,64]{3,1,4,2,0:T(4,128)(2,1)}), bf16[4,4,2,128,64]{3,1,4,2,0:T(4,128)(2,1)S(1)}, u32[]{:S(2)}, u32[]{:S(2)}) async-start(bf16[4,4,2,128,64]{3,1,4,2,0:T(4,128)(2,1)} %copy.111), calls=%async_computation | async-start | bytes 1048576 | tf_op jit(solution)/shard_map/all_to_all | solution.py:173
  123.5 6.3 %copy-start.9 = (bf16[4,32,1792]{2,1,0:T(8,128)(2,1)S(1)}, bf16[4,32,1792]{2,1,0:T(8,128)(2,1)}, u32[]{:S(2)}) copy-start(bf16[4,32,1792]{2,1,0:T(8,128)(2,1)} %copy-done.8) | copy-start | bytes 1376260
  123.5 21.6 %all-gather.7.cloned.1.call-start = ((), (), s32[]{:S(2)}) async-start(), calls=%async_computation.3 | async-start | bytes 1310720 | tf_op jit(solution)/shard_map/all_gather | solution.py:67
  129.2 4.1 %copy-start.10 = (bf16[4,32,1792]{2,1,0:T(8,128)(2,1)S(1)}, bf16[4,32,1792]{2,1,0:T(8,128)(2,1)}, u32[]{:S(2)}) copy-start(bf16[4,32,1792]{2,1,0:T(8,128)(2,1)} %copy-done.8) | copy-start | bytes 1376260
  136.4 13.6 %copy-start.7 = (f32[128,1024]{1,0:T(8,128)S(1)}, f32[128,1024]{1,0:T(8,128)}, u32[]{:S(2)}) copy-start(f32[128,1024]{1,0:T(8,128)} %fusion.4) | copy-start | bytes 1572868
  145.1 4.6 %copy-start.17 = (bf16[1,1,128,64]{2,0,3,1:T(2,128)(2,1)S(1)}, bf16[1,1,128,64]{2,0,3,1:T(2,128)(2,1)}, u32[]{:S(2)}) copy-start(bf16[1,1,128,64]{2,0,3,1:T(2,128)(2,1)} %get-tuple-element.30) | copy-start | bytes 49156
  145.1 4.9 %copy-start.16 = (bf16[1,1,128,64]{2,0,3,1:T(2,128)(2,1)S(1)}, bf16[1,1,128,64]{2,0,3,1:T(2,128)(2,1)}, u32[]{:S(2)}) copy-start(bf16[1,1,128,64]{2,0,3,1:T(2,128)(2,1)} %get-tuple-element.23) | copy-start | bytes 49156
  145.1 5.7 %copy-start.5 = (f32[128,1024]{1,0:T(8,128)S(1)}, f32[128,1024]{1,0:T(8,128)}, u32[]{:S(2)}) copy-start(f32[128,1024]{1,0:T(8,128)} %fusion.8) | copy-start | bytes 1572868
  145.1 5.7 %copy-start.15 = (bf16[1,1,128,64]{2,0,3,1:T(2,128)(2,1)S(1)}, bf16[1,1,128,64]{2,0,3,1:T(2,128)(2,1)}, u32[]{:S(2)}) copy-start(bf16[1,1,128,64]{2,0,3,1:T(2,128)(2,1)} %get-tuple-element.24) | copy-start | bytes 49156
  145.1 5.9 %copy-start.14 = (bf16[1,1,128,64]{2,0,3,1:T(2,128)(2,1)S(1)}, bf16[1,1,128,64]{2,0,3,1:T(2,128)(2,1)}, u32[]{:S(2)}) copy-start(bf16[1,1,128,64]{2,0,3,1:T(2,128)(2,1)} %get-tuple-element.25) | copy-start | bytes 49156
  145.1 42.5 %slice-start = ((s8[14680064]{0:T(1024)(128)(4,1)}), s8[4194304]{0:T(1024)(128)(4,1)S(1)}, s32[]{:S(2)}) async-start(s8[14680064]{0:T(1024)(128)(4,1)} %bitcast.240), calls=%async_computation.4 | async-start | bytes 8388608
  149.7 3.4 %copy-start.13 = (bf16[1,1,128,64]{2,0,3,1:T(2,128)(2,1)S(1)}, bf16[1,1,128,64]{2,0,3,1:T(2,128)(2,1)}, u32[]{:S(2)}) copy-start(bf16[1,1,128,64]{2,0,3,1:T(2,128)(2,1)} %get-tuple-element.29) | copy-start | bytes 49156
  150.0 3.4 %copy-start.12 = (bf16[1,1,128,64]{2,0,3,1:T(2,128)(2,1)S(1)}, bf16[1,1,128,64]{2,0,3,1:T(2,128)(2,1)}, u32[]{:S(2)}) copy-start(bf16[1,1,128,64]{2,0,3,1:T(2,128)(2,1)} %get-tuple-element.28) | copy-start | bytes 49156
  150.3 3.8 %copy-start.6 = (f32[128,1024]{1,0:T(8,128)S(1)}, f32[128,1024]{1,0:T(8,128)}, u32[]{:S(2)}) copy-start(f32[128,1024]{1,0:T(8,128)} %fusion.16) | copy-start | bytes 1572868
  150.3 3.8 %copy-start.11 = (bf16[1,1,128,64]{2,0,3,1:T(2,128)(2,1)S(1)}, bf16[1,1,128,64]{2,0,3,1:T(2,128)(2,1)}, u32[]{:S(2)}) copy-start(bf16[1,1,128,64]{2,0,3,1:T(2,128)(2,1)} %get-tuple-element.27) | copy-start | bytes 49156
  150.4 9.2 %collective-permute-start.6 = (bf16[64,2048]{1,0:T(8,128)(2,1)S(1)}, bf16[64,2048]{1,0:T(8,128)(2,1)S(1)}, u32[]{:S(2)}, u32[]{:S(2)}) collective-permute-start(bf16[64,2048]{1,0:T(8,128)(2,1)S(1)} %pad_maximum_fusion.3), channel_id=1, source_target_pairs={{0,2},{2,0},{1,3},{3,1},{4,6},{6,4},{5,7},{7,5},{8,10},{10,8},{9,1... | collective-permute-start | bytes 786440 | tf_op jit(solution)/shard_map/ppermute | solution.py:189
  150.8 36.8 %slice-start.1 = ((s8[14680064]{0:T(1024)(128)(4,1)}), s8[4194304]{0:T(1024)(128)(4,1)S(1)}, s32[]{:S(2)}) async-start(s8[14680064]{0:T(1024)(128)(4,1)} %bitcast.240), calls=%async_computation.5 | async-start | bytes 8388608
  151.4 13.8 %collective-permute-start.4 = (bf16[64,2048]{1,0:T(8,128)(2,1)S(1)}, bf16[64,2048]{1,0:T(8,128)(2,1)S(1)}, u32[]{:S(2)}, u32[]{:S(2)}) collective-permute-start(bf16[64,2048]{1,0:T(8,128)(2,1)S(1)} %pad_maximum_fusion.2), channel_id=1, source_target_pairs={{0,2},{2,0},{1,3},{3,1},{4,6},{6,4},{5,7},{7,5},{8,10},{10,8},{9,1... | collective-permute-start | bytes 786440 | tf_op jit(solution)/shard_map/ppermute | solution.py:189
  153.7 23.3 %collective-permute-start = (bf16[64,2048]{1,0:T(8,128)(2,1)S(1)}, bf16[64,2048]{1,0:T(8,128)(2,1)S(1)}, u32[]{:S(2)}, u32[]{:S(2)}) collective-permute-start(bf16[64,2048]{1,0:T(8,128)(2,1)S(1)} %pad_maximum_fusion), channel_id=1, source_target_pairs={{0,2},{2,0},{1,3},{3,1},{4,6},{6,4},{5,7},{7,5},{8,10},{10,8},{9,1... | collective-permute-start | bytes 786440 | tf_op jit(solution)/shard_map/ppermute | solution.py:189
  154.4 33.2 %slice-start.2 = ((s8[14680064]{0:T(1024)(128)(4,1)}), s8[4194304]{0:T(1024)(128)(4,1)S(1)}, s32[]{:S(2)}) async-start(s8[14680064]{0:T(1024)(128)(4,1)} %bitcast.240), calls=%async_computation.6 | async-start | bytes 8388608
  154.7 21.7 %collective-permute-start.2 = (bf16[64,2048]{1,0:T(8,128)(2,1)S(1)}, bf16[64,2048]{1,0:T(8,128)(2,1)S(1)}, u32[]{:S(2)}, u32[]{:S(2)}) collective-permute-start(bf16[64,2048]{1,0:T(8,128)(2,1)S(1)} %pad_maximum_fusion.1), channel_id=1, source_target_pairs={{0,2},{2,0},{1,3},{3,1},{4,6},{6,4},{5,7},{7,5},{8,10},{10,8},{9,1... | collective-permute-start | bytes 786440 | tf_op jit(solution)/shard_map/ppermute | solution.py:189
  159.6 25.2 %copy-start.27 = (f32[128]{0:T(128)S(1)}, f32[128]{0:T(128)}, u32[]{:S(2)}) copy-start(f32[128]{0:T(128)} %get-tuple-element.47) | copy-start | bytes 1540
  159.7 29.3 %collective-permute-start.7 = (bf16[64,1024]{1,0:T(8,128)(2,1)S(1)}, bf16[64,1024]{1,0:T(8,128)(2,1)S(1)}, u32[]{:S(2)}, u32[]{:S(2)}) collective-permute-start(bf16[64,1024]{1,0:T(8,128)(2,1)S(1)} %fusion.102), channel_id=1, source_target_pairs={{0,2},{2,0},{1,3},{3,1},{4,6},{6,4},{5,7},{7,5},{8,10},{10,8},{9,1... | collective-permute-start | bytes 393224 | tf_op jit(solution)/shard_map/ppermute | solution.py:194
  165.4 23.0 %collective-permute-start.5 = (bf16[64,1024]{1,0:T(8,128)(2,1)S(1)}, bf16[64,1024]{1,0:T(8,128)(2,1)S(1)}, u32[]{:S(2)}, u32[]{:S(2)}) collective-permute-start(bf16[64,1024]{1,0:T(8,128)(2,1)S(1)} %fusion.104), channel_id=1, source_target_pairs={{0,2},{2,0},{1,3},{3,1},{4,6},{6,4},{5,7},{7,5},{8,10},{10,8},{9,1... | collective-permute-start | bytes 393224 | tf_op jit(solution)/shard_map/ppermute | solution.py:194
  176.5 11.1 %slice-start.3 = ((s8[14680064]{0:T(1024)(128)(4,1)}), s8[2097152]{0:T(1024)(128)(4,1)S(1)}, s32[]{:S(2)}) async-start(s8[14680064]{0:T(1024)(128)(4,1)} %bitcast.240), calls=%async_computation.7 | async-start | bytes 4194304
  176.6 11.0 %copy-start.26 = (f32[128]{0:T(128)S(1)}, f32[128]{0:T(128)}, u32[]{:S(2)}) copy-start(f32[128]{0:T(128)} %get-tuple-element.48) | copy-start | bytes 1540
  176.6 8.2 %collective-permute-start.3 = (bf16[64,1024]{1,0:T(8,128)(2,1)S(1)}, bf16[64,1024]{1,0:T(8,128)(2,1)S(1)}, u32[]{:S(2)}, u32[]{:S(2)}) collective-permute-start(bf16[64,1024]{1,0:T(8,128)(2,1)S(1)} %fusion.106), channel_id=1, source_target_pairs={{0,2},{2,0},{1,3},{3,1},{4,6},{6,4},{5,7},{7,5},{8,10},{10,8},{9,1... | collective-permute-start | bytes 393224 | tf_op jit(solution)/shard_map/ppermute | solution.py:194
  177.2 10.4 %collective-permute-start.1 = (bf16[64,1024]{1,0:T(8,128)(2,1)S(1)}, bf16[64,1024]{1,0:T(8,128)(2,1)S(1)}, u32[]{:S(2)}, u32[]{:S(2)}) collective-permute-start(bf16[64,1024]{1,0:T(8,128)(2,1)S(1)} %fusion.108), channel_id=1, source_target_pairs={{0,2},{2,0},{1,3},{3,1},{4,6},{6,4},{5,7},{7,5},{8,10},{10,8},{9,1... | collective-permute-start | bytes 393224 | tf_op jit(solution)/shard_map/ppermute | solution.py:194
  187.5 0.8 copy-start.25
  188.3 0.7 copy-start.24
  189.1 18.0 %copy-start.1 = (bf16[1792,512]{1,0:T(8,128)(2,1)S(1)}, bf16[1792,512]{1,0:T(8,128)(2,1)}, u32[]{:S(2)}) copy-start(bf16[1792,512]{1,0:T(8,128)(2,1)} %param.17) | copy-start | bytes 5505028
Sparse Core Ops, SparseCore 0:
  126.4 18.6 all-gather.6

commit v2 on v1

--- a/solution.py
+++ b/solution.py
@@ -1,6 +1,8 @@
 import jax
 import jax.numpy as jnp
 from jax import lax
+from jax.experimental import pallas as pl
+from jax.experimental.pallas import tpu as pltpu
 from jax.sharding import PartitionSpec as P
 
 EPS = 1e-06
@@ -17,6 +19,90 @@
         terms.append(term.astype(BF16))
         value = value - term
     return terms
+
+
+def exchange(items, collective_id):
+    sizes = [[lax.axis_size(axis) for axis in axes] for _, axes, _ in items]
+    counts = []
+    for dims in sizes:
+        count = 1
+        for dim in dims:
+            count *= dim
+        counts.append(count)
+    greeted = max(range(len(items)), key=lambda i: counts[i])
+
+    def kernel(*refs):
+        number = len(items)
+        sources, targets = refs[:number], refs[number : 2 * number]
+        sends, receives = refs[2 * number : 3 * number], refs[3 * number : 4 * number]
+
+        def own(which):
+            place = 0
+            for axis, dim in zip(items[which][1], sizes[which]):
+                place = place * dim + lax.axis_index(axis)
+            return place
+
+        def device(which, place):
+            found = {}
+            for axis, dim in reversed(list(zip(items[which][1], sizes[which]))):
+                found[axis] = lax.rem(place, dim)
+                place = place // dim
+            return found
+
+        barrier = pltpu.get_barrier_semaphore()
+        me = own(greeted)
+        for offset in range(1, counts[greeted]):
+            pl.semaphore_signal(
+                barrier,
+                inc=1,
+                device_id=device(greeted, lax.rem(me + offset, counts[greeted])),
+                device_id_type=pl.DeviceIdType.MESH,
+            )
+        pl.semaphore_wait(barrier, counts[greeted] - 1)
+        copies = []
+        for which in range(number):
+            me, count = own(which), counts[which]
+            for offset in range(1, count):
+                peer = lax.rem(me + offset, count)
+                source = sources[which]
+                if items[which][2] == "scatter":
+                    source = source.at[peer]
+                copy = pltpu.make_async_remote_copy(
+                    src_ref=source,
+                    dst_ref=targets[which].at[me],
+                    send_sem=sends[which].at[offset - 1],
+                    recv_sem=receives[which].at[offset - 1],
+                    device_id=device(which, peer),
+                    device_id_type=pl.DeviceIdType.MESH,
+                )
+                copy.start()
+                copies.append(copy)
+        for which in range(number):
+            me = own(which)
+            if items[which][2] == "scatter":
+                targets[which][me] = sources[which][me]
+            else:
+                targets[which][me] = sources[which][...]
+        for copy in copies:
+            copy.wait()
+
+    shapes = [
+        array.shape if kind == "scatter" else (count, *array.shape)
+        for (array, _, kind), count in zip(items, counts)
+    ]
+    semaphores = [pltpu.SemaphoreType.DMA((max(1, count - 1),)) for count in counts]
+    return pl.pallas_call(
+        kernel,
+        out_shape=[
+            jax.ShapeDtypeStruct(shape, array.dtype) for shape, (array, _, _) in zip(shapes, items)
+        ],
+        in_specs=[pl.BlockSpec(memory_space=pltpu.VMEM)] * len(items),
+        out_specs=[pl.BlockSpec(memory_space=pltpu.VMEM)] * len(items),
+        scratch_shapes=semaphores + semaphores,
+        compiler_params=pltpu.CompilerParams(
+            collective_id=collective_id, has_side_effects=True, vmem_limit_bytes=16 << 20
+        ),
+    )(*[array for array, _, _ in items])
 
 
 def shards(
@@ -70,8 +156,7 @@
         expert_ids.reshape(batch, -1)[:, :, None]
         == jnp.arange(expert_count, dtype=jnp.int32)[None, None, :],
         axis=1,
-    ).astype(BF16)
-    chosen_all = lax.all_gather(chosen, "expert", axis=0, tiled=False)
+    ).astype(F32)
 
     tokens = inputs.reshape(batch, width)
     tokens_wide = tokens.astype(F32)
@@ -81,7 +166,8 @@
     normed_cols = (
         token_cols.astype(F32) * lax.rsqrt(square_mean + EPS) * gain_piece
     ).astype(BF16)
-    projected = lax.psum(jnp.dot(normed_cols, qkv_weight, preferred_element_type=F32), "tensor")
+    projected = jnp.dot(normed_cols, qkv_weight, preferred_element_type=F32)
+    projected = jnp.sum(exchange([(projected, ("tensor",), "gather")], 0)[0], axis=0)
     queries = projected[:, :lat].astype(BF16).reshape(steps, rows_here, lat)
     fresh = projected[:, lat:].astype(BF16).reshape(steps, rows_here, lat)
 
@@ -104,7 +190,9 @@
         ),
         axis=2,
     )
-    parts = lax.all_gather(packed, "tensor", axis=0, tiled=False)
+    packed = packed.reshape(rows_here * steps, lat + 128)
+    parts = exchange([(packed, ("tensor",), "gather")], 1)[0]
+    parts = parts.reshape(tensor_count, rows_here, steps, lat + 128)
     part_sums, part_tops, part_totals = (
         parts[..., :lat],
         parts[..., lat],
@@ -138,13 +226,19 @@
     )
     partial_squares = jnp.sum(middle_wide * middle_wide, axis=-1, keepdims=True)
     statistics = jnp.concatenate(
-        (partial_logits, jnp.broadcast_to(partial_squares, (batch, 128 - expert_count))), axis=1
-    )
-    statistics = lax.all_gather(statistics, ("expert", "tensor"), axis=0, tiled=False)
+        (
+            partial_logits,
+            jnp.where(tensor_index == 0, chosen, 0.0),
+            jnp.broadcast_to(partial_squares, (batch, 128 - 2 * expert_count)),
+        ),
+        axis=1,
+    )
+    statistics, middle_all = exchange(
+        [(statistics, ("expert", "tensor"), "gather"), (middle, ("expert",), "gather")], 2
+    )
     statistics = jnp.sum(
         statistics.reshape(shard_count, tensor_count, batch, 128), axis=1
     )
-    middle_all = lax.all_gather(middle, "expert", axis=0, tiled=False)
 
     def turned(value):
         if not paired:
@@ -155,7 +249,7 @@
 
     statistics = turned(statistics).reshape(total_rows, 128)
     rows_all = turned(middle_all).reshape(total_rows, part_cols)
-    mask_all = turned(chosen_all).reshape(total_rows, expert_count).astype(F32)
+    mask_all = statistics[:, expert_count : 2 * expert_count]
 
     inverse = lax.rsqrt(statistics[:, 127:] / width + EPS)
     routed_in = (rows_all.astype(F32) * inverse * gain_cols).astype(BF16)
@@ -165,33 +259,33 @@
         route, shard_index * experts_here, experts_here, 1
     ).astype(F32)
 
-    low = jnp.einsum("nd,sxdr->sxnr", routed_in, pool_left, preferred_element_type=F32)
-    low_sent = jnp.einsum(
-        "es,sxnr->exnr", serves, low.astype(BF16), preferred_element_type=F32
-    ).astype(BF16)
-    low_sent = low_sent.reshape(shard_count, experts_here, 2, total_rows, rank)
-    low_got = lax.all_to_all(low_sent, "expert", split_axis=0, concat_axis=0, tiled=True)
+    low = jnp.einsum("nd,sxdr->snxr", routed_in, pool_left, preferred_element_type=F32)
+    low = low.astype(BF16).reshape(slots_here, total_rows, 2 * rank)
+    low_sent = jnp.einsum("es,snq->enq", serves, low, preferred_element_type=F32).astype(BF16)
+    low_sent = low_sent.reshape(shard_count, experts_here * total_rows, 2 * rank)
+    low_got = exchange([(low_sent, ("expert",), "scatter")], 3)[0]
     low_own = jnp.sum(low_got.astype(F32), axis=0).astype(BF16)
-
-    exchange = [(0, 1), (1, 0)]
+    low_own = low_own.reshape(experts_here, total_rows, 2, rank)
+
+    swap = [(0, 1), (1, 0)]
     mixture = jnp.zeros((total_rows, part_cols), F32)
     for expert in range(experts_here):
         partial = [
             jnp.dot(routed_in, weight[expert], preferred_element_type=F32)
             + jnp.dot(
-                low_own[expert, which], right_full[expert, which], preferred_element_type=F32
+                low_own[expert, :, which], right_full[expert, which], preferred_element_type=F32
             )
             for which, weight in enumerate((gate_weight, up_weight))
         ]
         if paired:
             half_rows = total_rows // 2
             sent = jnp.concatenate([value[half_rows:].astype(BF16) for value in partial], axis=1)
-            got = lax.ppermute(sent, "tensor", exchange).astype(F32)
+            got = lax.ppermute(sent, "tensor", swap).astype(F32)
             gate = partial[0][:half_rows] + got[:, :ffw]
             up = partial[1][:half_rows] + got[:, ffw:]
             hidden = (jax.nn.silu(gate) * up).astype(BF16)
             hidden = jnp.concatenate(
-                (hidden, lax.ppermute(hidden, "tensor", exchange)), axis=0
+                (hidden, lax.ppermute(hidden, "tensor", swap)), axis=0
             )
         else:
             summed = lax.psum_scatter(
@@ -203,7 +297,7 @@
         mixture = mixture + route_here[:, expert : expert + 1] * answered.astype(F32)
 
     returned = turned(mixture.astype(BF16).reshape(shard_count, batch, part_cols))
-    returned = lax.all_to_all(returned, "expert", split_axis=0, concat_axis=0, tiled=True)
+    returned = exchange([(returned, ("expert",), "scatter")], 4)[0]
     outputs = (middle_wide + jnp.sum(returned.astype(F32), axis=0)).astype(BF16)
     return outputs.reshape(steps, rows_here, part_cols)
 

time: 215 us -> 172 us (0.80)
  blocking collectives: 91.9 us -> 0 us
  Pallas kernels: 0 us -> 56.1 us
  starting transfers between devices: 17.3 us -> 13.7 us
  waiting for transfers between devices: 32.6 us -> 29.4 us
    all_gather x4 -> x0, blocking collectives: 66.4 us -> none  [the longest x1 30.5 us: shards(): lax.all_gather(statistics, ('expert', 'tensor'), axis=0, tiled=False)]
    pallas_call x0 -> x5, Pallas kernels: none -> 56.1 us  [exchange(): pl.pallas_call(kernel, out_shape=[jax.ShapeDtypeStruct(shape, array.dtype...]
    all_to_all x1 -> x0, blocking collectives: 16.5 us -> none  [shards(): lax.all_to_all(returned, 'expert', split_axis=0, concat_axis=0, tiled=True)]
    psum x1 -> x0, blocking collectives: 9 us -> none  [shards(): lax.psum(jnp.dot(normed_cols, qkv_weight, preferred_element_type=F32), 't...]
    all_to_all x1 -> x0, starting transfers between devices: 3.48 us -> none  [shards(): lax.all_to_all(low_sent, 'expert', split_axis=0, concat_axis=0, tiled=True)]
    all_gather x1, waiting for transfers between devices: 7.81 us -> 4.67 us  [shards(): right_full = lax.all_gather(right_own, ('dp', 'tensor'), axis=3, tiled=True)]
    dot_general x10 -> x11, matrix products: 6.76 us -> 3.97 us  [the longest x8 1.98 us: shards(): jnp.dot(low_own[expert, :, which], right_full[expert, which], preferred_e...]
  transfers between devices with their start and end apart: 11 -> 10, of which waited for: 5 -> 5; matrix products, arithmetic and copies ran while one was open for 21% -> 23% of each run, Pallas kernels for 0% -> 26%
where the time goes in v2:
time: 172 us; the launch traced here: 171 us
  Pallas kernels  56.1 us (33%)
  matrix products  36.2 us (21%)
  waiting for transfers between devices  29.4 us (17%)
  local copies, waits for them, and re-layouts  15.4 us (9%)
  between operations  14.3 us (8%)
  starting transfers between devices  13.7 us (8%)
  other arithmetic  6.14 us (4%)
    pallas_call x5, Pallas kernels, exchange(): pl.pallas_call(kernel, out_shape=[jax.ShapeDtypeStruct(shape, array.dtype...  56.1 us
    dot_general x8, matrix products, shards(): jnp.dot(routed_in, weight[expert], preferred_element_type=F32)  25 us
    ppermute x4, waiting for transfers between devices, shards(): got = lax.ppermute(sent, 'tensor', swap).astype(F32)  18.8 us
    all_to_all x1, starting transfers between devices, shards(): lax.all_to_all(right_sent, 'expert', split_axis=0, concat_axis=0, tiled=T...  6.32 us
    ppermute x4, waiting for transfers between devices, shards(): lax.ppermute(hidden, 'tensor', swap)  5.94 us
    dot_general x4, matrix products, shards(): jnp.dot(hidden, down_weight[expert], preferred_element_type=F32)  4.74 us
    slice x1, local copies, waits for them, and re-layouts, shards(): right_full[expert, which]  4.7 us
    all_gather x1, waiting for transfers between devices, shards(): right_full = lax.all_gather(right_own, ('dp', 'tensor'), axis=3, tiled=True)  4.67 us
  transfers between devices with their start and end apart: 10, of which 5 were waited for; matrix products, arithmetic and copies ran while one was open for 23% of the time, Pallas kernels for 26%

profile of v2, /device:TPU:0, one launch (start us, length us, event | category | flops | bytes accessed | tf_op | source)
XLA Modules:
  0.0 171.2 jit_solution(15284215645065833652)
XLA Ops:
  6.5 1.2 constant_dynamic-slice_fusion
  7.8 1.3 convolution_convert_fusion
  9.1 1.1 reshape.230
  10.2 2.7 %copy.139 = bf16[4,4,2,64,256]{4,1,3,2,0:T(4,128)(2,1)} copy(bf16[4,4,2,64,256]{4,1,0,3,2:T(4,128)(2,1)} %reshape.230) | data formatting | bytes 2097152 | tf_op jit(solution)/shard_map/reshape | solution.py:150
  12.9 6.3 %all-to-all-start = ((bf16[4,4,2,64,256]{4,1,3,2,0:T(4,128)(2,1)}), bf16[4,4,2,64,256]{4,1,3,2,0:T(4,128)(2,1)}, u32[]{:S(2)}, u32[]{:S(2)}) async-start(bf16[4,4,2,64,256]{4,1,3,2,0:T(4,128)(2,1)} %copy.139), calls=%async_computation | async-start | bytes 2097152 | tf_op jit(solution)/shard_map/all_to_all | solution.py:151
  19.6 0.5 fusion.131.refs_0_
  20.0 4.3 %shard_map.145 = f32[2,32,512]{2,1,0:T(8,128)S(1)} custom-call(f32[32,512]{1,0:T(8,128)S(1)} %fusion.131.refs_0_), custom_call_target="tpu_custom_call" | custom-call | tf_op jit(solution)/shard_map/pallas_call | solution.py:94
  24.4 0.4 fusion.165
  25.7 4.1 %shard_map.146 = f32[2,32,384]{2,1,0:T(8,128)S(1)} custom-call(f32[32,384]{1,0:T(8,128)S(1)} %reshape.223.refs_0_), custom_call_target="tpu_custom_call" | custom-call | tf_op jit(solution)/shard_map/pallas_call | solution.py:94
  31.4 0.4 fusion.113
  32.2 24.1 %shard_map.147 = (f32[8,32,128]{2,1,0:T(8,128)S(1)}, bf16[4,32,1792]{2,1,0:T(8,128)(2,1)S(1)}) custom-call(f32[32,128]{1,0:T(8,128)S(1)} %pad_maximum_fusion.6.refs_0_, bf16[32,1792]{1,0:T(8,128)(2,1)S(1)} %get-tuple-element.54.refs_1_), custom_call_target="tpu_custom_call" | custom-call | tf_op jit(solution)/shard_map/pallas_call | solution.py:94
  57.1 1.9 %copy-done.2 = bf16[8,2,1792,64]{2,3,1,0:T(8,128)(2,1)S(1)} copy-done((bf16[8,2,1792,64]{2,3,1,0:T(8,128)(2,1)S(1)}, bf16[8,2,1792,64]{2,3,1,0:T(8,128)(2,1)}, u32[]{:S(2)}) %copy-start.2) | copy-done | bytes 3670040
  59.0 1.1 convolution_convert_fusion.2
  60.3 0.4 convolution_convert_fusion.1
  60.9 12.7 %shard_map.148 = bf16[4,512,128]{2,1,0:T(8,128)(2,1)S(1)} custom-call(bf16[4,512,128]{2,1,0:T(8,128)(2,1)S(1)} %bitcast.210), custom_call_target="tpu_custom_call" | custom-call | tf_op jit(solution)/shard_map/pallas_call | solution.py:94
  73.8 0.9 fusion.190
  74.9 2.7 %fusion.2 = f32[128,1024]{1,0:T(8,128)S(1)} fusion(bf16[128,1792]{1,0:T(8,128)(2,1)S(1)} %bitcast.219, bf16[4,1792,1024]{2,1,0:T(8,128)(2,1)} %param.25), kind=kOutput, calls=%fused_computation.2 | convolution fusion | flops 469762048 | bytes 4653056 | tf_op jit(solution)/shard_map/dot_general | solution.py:274
  77.6 3.5 %fusion.8 = f32[128,1024]{1,0:T(8,128)} fusion(bf16[128,1792]{1,0:T(8,128)(2,1)S(1)} %bitcast.220, bf16[4,1792,1024]{2,1,0:T(8,128)(2,1)} %param.25), kind=kOutput, calls=%fused_computation.8 | convolution fusion | flops 469762048 | bytes 4653056 | tf_op jit(solution)/shard_map/dot_general | solution.py:274
  81.1 3.5 %fusion.4 = f32[128,1024]{1,0:T(8,128)} fusion(bf16[128,1792]{1,0:T(8,128)(2,1)S(1)} %bitcast.221, bf16[4,1792,1024]{2,1,0:T(8,128)(2,1)} %param.24), kind=kOutput, calls=%fused_computation.4 | convolution fusion | flops 469762048 | bytes 4653056 | tf_op jit(solution)/shard_map/dot_general | solution.py:274
  84.6 2.7 %fusion.10 = f32[128,1024]{1,0:T(8,128)S(1)} fusion(bf16[128,1792]{1,0:T(8,128)(2,1)S(1)} %bitcast.222, bf16[4,1792,1024]{2,1,0:T(8,128)(2,1)} %param.24), kind=kOutput, calls=%fused_computation.10 | convolution fusion | flops 469762048 | bytes 4653056 | tf_op jit(solution)/shard_map/dot_general | solution.py:274
  87.3 2.5 %reduce_sum.157 = bf16[4,2,64,256]{3,0,2,1:T(4,128)(2,1)} reduce(bf16[4,4,2,64,256]{4,1,3,2,0:T(4,128)(2,1)} %all-to-all-done, bf16[]{:T(256)} %constant.55.clone.1), dimensions={0}, to_apply=%region_17.18 | reduce | flops 393216 | bytes 1310722 | tf_op jit(solution)/shard_map/reduce_sum | solution.py:152
  89.8 0.6 slice_bitcast_fusion
  90.4 3.5 %fusion.22 = f32[128,1024]{1,0:T(8,128)} fusion(bf16[128,1792]{1,0:T(8,128)(2,1)S(1)} %bitcast.223, bf16[4,1792,1024]{2,1,0:T(8,128)(2,1)} %param.24), kind=kOutput, calls=%fused_computation.22 | convolution fusion | flops 469762048 | bytes 4653056 | tf_op jit(solution)/shard_map/dot_general | solution.py:274
  93.9 3.5 %fusion.20 = f32[128,1024]{1,0:T(8,128)} fusion(bf16[128,1792]{1,0:T(8,128)(2,1)S(1)} %bitcast.224, bf16[4,1792,1024]{2,1,0:T(8,128)(2,1)} %param.25), kind=kOutput, calls=%fused_computation.20 | convolution fusion | flops 469762048 | bytes 4653056 | tf_op jit(solution)/shard_map/dot_general | solution.py:274
  97.4 3.0 %fusion.16 = f32[128,1024]{1,0:T(8,128)S(1)} fusion(bf16[128,1792]{1,0:T(8,128)(2,1)} %bitcast.225, bf16[4,1792,1024]{2,1,0:T(8,128)(2,1)} %param.24), kind=kOutput, calls=%fused_computation.16 | convolution fusion | flops 469762048 | bytes 4653056 | tf_op jit(solution)/shard_map/dot_general | solution.py:274
  100.5 2.7 %fusion.14 = f32[128,1024]{1,0:T(8,128)S(1)} fusion(bf16[128,1792]{1,0:T(8,128)(2,1)S(1)} %bitcast.226, bf16[4,1792,1024]{2,1,0:T(8,128)(2,1)} %param.25), kind=kOutput, calls=%fused_computation.14 | convolution fusion | flops 469762048 | bytes 4653056 | tf_op jit(solution)/shard_map/dot_general | solution.py:274
  103.1 4.7 %all-gather.2.cloned.1.call-done = bf16[4,2,64,1024]{3,0,2,1:T(4,128)(2,1)} async-done(((bf16[4,2,64,256]{3,0,2,1:T(4,128)(2,1)}), bf16[4,2,64,1024]{3,0,2,1:T(4,128)(2,1)}) %all-gather.2.cloned.1.call-update) | async-done | bytes 1048592 | tf_op jit(solution)/shard_map/all_gather | solution.py:153
  107.8 4.7 %fusion.187 = (bf16[1,1,64,1024]{3,0,2,1:T(2,128)(2,1)S(1)}, bf16[1,1,64,1024]{3,0,2,1:T(2,128)(2,1)S(1)}, bf16[1,1,64,1024]{3,0,2,1:T(2,128)(2,1)S(1)}, bf16[1,...) fusion(bf16[4,2,64,1024]{3,0,2,1:T(4,128)(2,1)} %all-gather.2.c, ...), kind=kLoop, calls=%fused_computation.238 | loop fusion | bytes 2097152 | tf_op jit(solution)/shard_map/slice | solution.py:276
  113.2 0.4 collective-permute-start.6
  114.2 1.8 %collective-permute-start.4 = (bf16[64,2048]{1,0:T(8,128)(2,1)S(1)}, bf16[64,2048]{1,0:T(8,128)(2,1)S(1)}, u32[]{:S(2)}, u32[]{:S(2)}) collective-permute-start(bf16[64,2048]{1,0:T(8,128)(2,1)S(1)} %pad_maximum_fusion.2), channel_id=1, source_target_pairs={{0,2},{2,0},{1,3},{3,1},{4,6},{6,4},{5,7},{7,5},{8,10},{10,8},{9,1... | collective-permute-start | bytes 786440 | tf_op jit(solution)/shard_map/ppermute | solution.py:283
  116.0 0.3 convolution_add_fusion.8
  116.3 0.3 convolution_add_fusion.7
  116.6 0.4 collective-permute-start
  117.6 1.8 %collective-permute-start.2 = (bf16[64,2048]{1,0:T(8,128)(2,1)S(1)}, bf16[64,2048]{1,0:T(8,128)(2,1)S(1)}, u32[]{:S(2)}, u32[]{:S(2)}) collective-permute-start(bf16[64,2048]{1,0:T(8,128)(2,1)S(1)} %pad_maximum_fusion.1), channel_id=1, source_target_pairs={{0,2},{2,0},{1,3},{3,1},{4,6},{6,4},{5,7},{7,5},{8,10},{10,8},{9,1... | collective-permute-start | bytes 786440 | tf_op jit(solution)/shard_map/ppermute | solution.py:283
  119.4 3.0 %collective-permute-done.6 = bf16[64,2048]{1,0:T(8,128)(2,1)S(1)} collective-permute-done((bf16[64,2048]{1,0:T(8,128)(2,1)S(1)}, bf16[64,2048]{1,0:T(8,128)(2,1)S(1)}, u32[]{:S(2)}, u32[]{:S(2)}) %collective-permute-start.6) | collective-permute-done | bytes 262176 | tf_op jit(solution)/shard_map/ppermute | solution.py:283
  122.6 0.4 collective-permute-start.7
  123.0 5.1 %collective-permute-done.4 = bf16[64,2048]{1,0:T(8,128)(2,1)S(1)} collective-permute-done((bf16[64,2048]{1,0:T(8,128)(2,1)S(1)}, bf16[64,2048]{1,0:T(8,128)(2,1)S(1)}, u32[]{:S(2)}, u32[]{:S(2)}) %collective-permute-start.4) | collective-permute-done | bytes 262176 | tf_op jit(solution)/shard_map/ppermute | solution.py:283
  128.2 0.4 collective-permute-start.5
  128.6 10.7 %collective-permute-done.2 = bf16[64,2048]{1,0:T(8,128)(2,1)S(1)} collective-permute-done((bf16[64,2048]{1,0:T(8,128)(2,1)S(1)}, bf16[64,2048]{1,0:T(8,128)(2,1)S(1)}, u32[]{:S(2)}, u32[]{:S(2)}) %collective-permute-start.2) | collective-permute-done | bytes 262176 | tf_op jit(solution)/shard_map/ppermute | solution.py:283
  139.4 0.4 collective-permute-start.3
  140.0 1.8 %collective-permute-start.1 = (bf16[64,1024]{1,0:T(8,128)(2,1)S(1)}, bf16[64,1024]{1,0:T(8,128)(2,1)S(1)}, u32[]{:S(2)}, u32[]{:S(2)}) collective-permute-start(bf16[64,1024]{1,0:T(8,128)(2,1)S(1)} %fusion.97), channel_id=1, source_target_pairs={{0,2},{2,0},{1,3},{3,1},{4,6},{6,4},{5,7},{7,5},{8,10},{10,8},{9,1... | collective-permute-start | bytes 393224 | tf_op jit(solution)/shard_map/ppermute | solution.py:288
  141.8 5.9 %collective-permute-done.3 = bf16[64,1024]{1,0:T(8,128)(2,1)S(1)} collective-permute-done((bf16[64,1024]{1,0:T(8,128)(2,1)S(1)}, bf16[64,1024]{1,0:T(8,128)(2,1)S(1)}, u32[]{:S(2)}, u32[]{:S(2)}) %collective-permute-start.3) | collective-permute-done | bytes 131104 | tf_op jit(solution)/shard_map/ppermute | solution.py:288
  147.7 2.7 %fusion.72 = f32[128,1792]{1,0:T(8,128)S(1)} fusion(bf16[4,1024,1792]{2,1,0:T(8,128)(2,1)} %param.26, f32[128]{0:T(128)S(1)} %copy-done.27, bf16[64,1024]{1,0:T(8,128)(2,1)S(1)} %collective-permute-done.3, bf16[64,1024]{1,0:T(8,128)(2,1)S(1)} %fusion.95), kind=kOutput, calls=%fused_computation.48 | convolution fusion | flops 470974464 | bytes 4850176 | tf_op jit(solution)/shard_map/dot_general | solution.py:296
  150.5 0.7 fusion.81
  151.2 0.7 fusion.66
  151.9 0.7 fusion.57
  152.7 10.9 %shard_map.149 = bf16[4,32,1792]{2,1,0:T(8,128)(2,1)S(1)} custom-call(bf16[4,32,1792]{2,1,0:T(8,128)(2,1)S(1)} %maximum_select_fusion.1.refs_0_), custom_call_target="tpu_custom_call" | custom-call | tf_op jit(solution)/shard_map/pallas_call | solution.py:94
  163.7 0.7 fusion.114
  (166 shorter events, 7.2 us)
Async XLA Ops:
  6.5 13.0 %copy-start = (bf16[1792,512]{1,0:T(8,128)(2,1)S(1)}, bf16[1792,512]{1,0:T(8,128)(2,1)}, u32[]{:S(2)}) copy-start(bf16[1792,512]{1,0:T(8,128)(2,1)} %param.17) | copy-start | bytes 5505028
  7.8 11.5 %copy-start.5 = (bf16[2,16,3584]{2,1,0:T(8,128)(2,1)S(1)}, bf16[2,16,3584]{2,1,0:T(8,128)(2,1)}, u32[]{:S(2)}) copy-start(bf16[2,16,3584]{2,1,0:T(8,128)(2,1)} %param.15) | copy-start | bytes 688132
  7.8 11.7 %copy-start.20 = (f32[3584]{0:T(1024)S(1)}, f32[3584]{0:T(1024)}, u32[]{:S(2)}) copy-start(f32[3584]{0:T(1024)} %param.16) | copy-start | bytes 43012
  10.2 14.2 %copy-start.3 = (bf16[16,128,256]{2,1,0:T(8,128)(2,1)S(1)}, bf16[16,128,256]{2,1,0:T(8,128)(2,1)}, u32[]{:S(2)}) copy-start(bf16[16,128,256]{2,1,0:T(8,128)(2,1)} %param.19) | copy-start | bytes 3145732
  10.2 14.6 %copy-start.23 = (s32[16]{0:T(128)S(1)}, s32[16]{0:T(128)}, u32[]{:S(2)}) copy-start(s32[16]{0:T(128)} %param.20) | copy-start | bytes 196
  12.9 74.4 %all-to-all-start = ((bf16[4,4,2,64,256]{4,1,3,2,0:T(4,128)(2,1)}), bf16[4,4,2,64,256]{4,1,3,2,0:T(4,128)(2,1)}, u32[]{:S(2)}, u32[]{:S(2)}) async-start(bf16[4,4,2,64,256]{4,1,3,2,0:T(4,128)(2,1)} %copy.139), calls=%async_computation | async-start | bytes 2097152 | tf_op jit(solution)/shard_map/all_to_all | solution.py:151
  19.2 11.8 %copy-start.21 = (f32[3584]{0:T(1024)S(1)}, f32[3584]{0:T(1024)}, u32[]{:S(2)}) copy-start(f32[3584]{0:T(1024)} %param.21) | copy-start | bytes 43012
  19.2 11.9 %copy-start.19 = (s32[2,16,8]{1,2,0:T(8,128)S(1)}, s32[2,16,8]{1,2,0:T(8,128)}, u32[]{:S(2)}) copy-start(s32[2,16,8]{1,2,0:T(8,128)} %param.23) | copy-start | bytes 3076
  19.2 88.6 %all-gather.2.cloned.1.call-start = ((), (), s32[]{:S(2)}) async-start(), calls=%async_computation.1 | async-start | bytes 1310720 | tf_op jit(solution)/shard_map/all_gather | solution.py:153
  19.6 12.2 %copy-start.18 = (bf16[3584,16]{0,1:T(8,128)(2,1)S(1)}, bf16[3584,16]{0,1:T(8,128)(2,1)}, u32[]{:S(2)}) copy-start(bf16[3584,16]{0,1:T(8,128)(2,1)} %param.22) | copy-start | bytes 344068
  20.0 11.4 %copy-start.4 = (bf16[256,1792]{1,0:T(8,128)(2,1)S(1)}, bf16[256,1792]{1,0:T(8,128)(2,1)}, u32[]{:S(2)}) copy-start(bf16[256,1792]{1,0:T(8,128)(2,1)} %param.18) | copy-start | bytes 2752516
  56.8 2.2 %copy-start.2 = (bf16[8,2,1792,64]{2,3,1,0:T(8,128)(2,1)S(1)}, bf16[8,2,1792,64]{2,3,1,0:T(8,128)(2,1)}, u32[]{:S(2)}) copy-start(bf16[8,2,1792,64]{2,3,1,0:T(8,128)(2,1)} %param.27) | copy-start | bytes 11010052
  57.0 36.9 %copy-start.10 = (bf16[4,32,1792]{2,1,0:T(8,128)(2,1)}, bf16[4,32,1792]{2,1,0:T(8,128)(2,1)S(1)}, u32[]{:S(2)}) copy-start(bf16[4,32,1792]{2,1,0:T(8,128)(2,1)S(1)} %get-tuple-element.9) | copy-start | bytes 1376260
  59.0 1.3 copy-start.22
  97.4 3.0 %copy-start.11 = (bf16[4,32,1792]{2,1,0:T(8,128)(2,1)S(1)}, bf16[4,32,1792]{2,1,0:T(8,128)(2,1)}, u32[]{:S(2)}) copy-start(bf16[4,32,1792]{2,1,0:T(8,128)(2,1)} %copy-done.10) | copy-start | bytes 1376260
  107.8 5.1 %copy-start.9 = (f32[128,1024]{1,0:T(8,128)S(1)}, f32[128,1024]{1,0:T(8,128)}, u32[]{:S(2)}) copy-start(f32[128,1024]{1,0:T(8,128)} %fusion.4) | copy-start | bytes 1572868
  107.8 5.1 %copy-start.17 = (bf16[1,128,1,64]{1,0,3,2:T(2,128)(2,1)S(1)}, bf16[1,128,1,64]{1,0,3,2:T(2,128)(2,1)}, u32[]{:S(2)}) copy-start(bf16[1,128,1,64]{1,0,3,2:T(2,128)(2,1)} %get-tuple-element.27) | copy-start | bytes 49156
  107.8 5.8 %copy-start.6 = (f32[128,1024]{1,0:T(8,128)S(1)}, f32[128,1024]{1,0:T(8,128)}, u32[]{:S(2)}) copy-start(f32[128,1024]{1,0:T(8,128)} %fusion.8) | copy-start | bytes 1572868
  107.8 5.8 %copy-start.16 = (bf16[1,128,1,64]{1,0,3,2:T(2,128)(2,1)S(1)}, bf16[1,128,1,64]{1,0,3,2:T(2,128)(2,1)}, u32[]{:S(2)}) copy-start(bf16[1,128,1,64]{1,0,3,2:T(2,128)(2,1)} %get-tuple-element.29) | copy-start | bytes 49156
  107.8 6.1 %copy-start.15 = (bf16[1,128,1,64]{1,0,3,2:T(2,128)(2,1)S(1)}, bf16[1,128,1,64]{1,0,3,2:T(2,128)(2,1)}, u32[]{:S(2)}) copy-start(bf16[1,128,1,64]{1,0,3,2:T(2,128)(2,1)} %get-tuple-element.30) | copy-start | bytes 49156
  107.8 42.6 %slice-start = ((s8[14680064]{0:T(1024)(128)(4,1)}), s8[4194304]{0:T(1024)(128)(4,1)S(1)}, s32[]{:S(2)}) async-start(s8[14680064]{0:T(1024)(128)(4,1)} %bitcast.230), calls=%async_computation.2 | async-start | bytes 8388608
  112.5 3.4 %copy-start.8 = (f32[128,1024]{1,0:T(8,128)S(1)}, f32[128,1024]{1,0:T(8,128)}, u32[]{:S(2)}) copy-start(f32[128,1024]{1,0:T(8,128)} %fusion.22) | copy-start | bytes 1572868
  112.6 3.4 %copy-start.14 = (bf16[1,128,1,64]{1,0,3,2:T(2,128)(2,1)S(1)}, bf16[1,128,1,64]{1,0,3,2:T(2,128)(2,1)}, u32[]{:S(2)}) copy-start(bf16[1,128,1,64]{1,0,3,2:T(2,128)(2,1)} %get-tuple-element.34) | copy-start | bytes 49156
  112.8 3.4 %copy-start.7 = (f32[128,1024]{1,0:T(8,128)S(1)}, f32[128,1024]{1,0:T(8,128)}, u32[]{:S(2)}) copy-start(f32[128,1024]{1,0:T(8,128)} %fusion.20) | copy-start | bytes 1572868
  112.8 3.4 %copy-start.13 = (bf16[1,128,1,64]{1,0,3,2:T(2,128)(2,1)S(1)}, bf16[1,128,1,64]{1,0,3,2:T(2,128)(2,1)}, u32[]{:S(2)}) copy-start(bf16[1,128,1,64]{1,0,3,2:T(2,128)(2,1)} %get-tuple-element.33) | copy-start | bytes 49156
  113.2 3.8 %copy-start.12 = (bf16[1,128,1,64]{1,0,3,2:T(2,128)(2,1)S(1)}, bf16[1,128,1,64]{1,0,3,2:T(2,128)(2,1)}, u32[]{:S(2)}) copy-start(bf16[1,128,1,64]{1,0,3,2:T(2,128)(2,1)} %get-tuple-element.32) | copy-start | bytes 49156
  113.2 9.2 %collective-permute-start.6 = (bf16[64,2048]{1,0:T(8,128)(2,1)S(1)}, bf16[64,2048]{1,0:T(8,128)(2,1)S(1)}, u32[]{:S(2)}, u32[]{:S(2)}) collective-permute-start(bf16[64,2048]{1,0:T(8,128)(2,1)S(1)} %pad_maximum_fusion.3), channel_id=1, source_target_pairs={{0,2},{2,0},{1,3},{3,1},{4,6},{6,4},{5,7},{7,5},{8,10},{10,8},{9,1... | collective-permute-start | bytes 786440 | tf_op jit(solution)/shard_map/ppermute | solution.py:283
  113.6 36.8 %slice-start.1 = ((s8[14680064]{0:T(1024)(128)(4,1)}), s8[4194304]{0:T(1024)(128)(4,1)S(1)}, s32[]{:S(2)}) async-start(s8[14680064]{0:T(1024)(128)(4,1)} %bitcast.230), calls=%async_computation.3 | async-start | bytes 8388608
  114.2 13.8 %collective-permute-start.4 = (bf16[64,2048]{1,0:T(8,128)(2,1)S(1)}, bf16[64,2048]{1,0:T(8,128)(2,1)S(1)}, u32[]{:S(2)}, u32[]{:S(2)}) collective-permute-start(bf16[64,2048]{1,0:T(8,128)(2,1)S(1)} %pad_maximum_fusion.2), channel_id=1, source_target_pairs={{0,2},{2,0},{1,3},{3,1},{4,6},{6,4},{5,7},{7,5},{8,10},{10,8},{9,1... | collective-permute-start | bytes 786440 | tf_op jit(solution)/shard_map/ppermute | solution.py:283
  116.6 23.3 %collective-permute-start = (bf16[64,2048]{1,0:T(8,128)(2,1)S(1)}, bf16[64,2048]{1,0:T(8,128)(2,1)S(1)}, u32[]{:S(2)}, u32[]{:S(2)}) collective-permute-start(bf16[64,2048]{1,0:T(8,128)(2,1)S(1)} %pad_maximum_fusion), channel_id=1, source_target_pairs={{0,2},{2,0},{1,3},{3,1},{4,6},{6,4},{5,7},{7,5},{8,10},{10,8},{9,1... | collective-permute-start | bytes 786440 | tf_op jit(solution)/shard_map/ppermute | solution.py:283
  117.2 33.2 %slice-start.2 = ((s8[14680064]{0:T(1024)(128)(4,1)}), s8[4194304]{0:T(1024)(128)(4,1)S(1)}, s32[]{:S(2)}) async-start(s8[14680064]{0:T(1024)(128)(4,1)} %bitcast.230), calls=%async_computation.4 | async-start | bytes 8388608
  117.6 21.7 %collective-permute-start.2 = (bf16[64,2048]{1,0:T(8,128)(2,1)S(1)}, bf16[64,2048]{1,0:T(8,128)(2,1)S(1)}, u32[]{:S(2)}, u32[]{:S(2)}) collective-permute-start(bf16[64,2048]{1,0:T(8,128)(2,1)S(1)} %pad_maximum_fusion.1), channel_id=1, source_target_pairs={{0,2},{2,0},{1,3},{3,1},{4,6},{6,4},{5,7},{7,5},{8,10},{10,8},{9,1... | collective-permute-start | bytes 786440 | tf_op jit(solution)/shard_map/ppermute | solution.py:283
  122.4 25.2 %copy-start.27 = (f32[128]{0:T(128)S(1)}, f32[128]{0:T(128)}, u32[]{:S(2)}) copy-start(f32[128]{0:T(128)} %get-tuple-element.51) | copy-start | bytes 1540
  122.6 29.3 %collective-permute-start.7 = (bf16[64,1024]{1,0:T(8,128)(2,1)S(1)}, bf16[64,1024]{1,0:T(8,128)(2,1)S(1)}, u32[]{:S(2)}, u32[]{:S(2)}) collective-permute-start(bf16[64,1024]{1,0:T(8,128)(2,1)S(1)} %fusion.91), channel_id=1, source_target_pairs={{0,2},{2,0},{1,3},{3,1},{4,6},{6,4},{5,7},{7,5},{8,10},{10,8},{9,1... | collective-permute-start | bytes 393224 | tf_op jit(solution)/shard_map/ppermute | solution.py:288
  128.2 23.0 %collective-permute-start.5 = (bf16[64,1024]{1,0:T(8,128)(2,1)S(1)}, bf16[64,1024]{1,0:T(8,128)(2,1)S(1)}, u32[]{:S(2)}, u32[]{:S(2)}) collective-permute-start(bf16[64,1024]{1,0:T(8,128)(2,1)S(1)} %fusion.93), channel_id=1, source_target_pairs={{0,2},{2,0},{1,3},{3,1},{4,6},{6,4},{5,7},{7,5},{8,10},{10,8},{9,1... | collective-permute-start | bytes 393224 | tf_op jit(solution)/shard_map/ppermute | solution.py:288
  139.3 11.1 %slice-start.3 = ((s8[14680064]{0:T(1024)(128)(4,1)}), s8[2097152]{0:T(1024)(128)(4,1)S(1)}, s32[]{:S(2)}) async-start(s8[14680064]{0:T(1024)(128)(4,1)} %bitcast.230), calls=%async_computation.5 | async-start | bytes 4194304
  139.4 11.0 %copy-start.26 = (f32[128]{0:T(128)S(1)}, f32[128]{0:T(128)}, u32[]{:S(2)}) copy-start(f32[128]{0:T(128)} %get-tuple-element.52) | copy-start | bytes 1540
  139.4 8.2 %collective-permute-start.3 = (bf16[64,1024]{1,0:T(8,128)(2,1)S(1)}, bf16[64,1024]{1,0:T(8,128)(2,1)S(1)}, u32[]{:S(2)}, u32[]{:S(2)}) collective-permute-start(bf16[64,1024]{1,0:T(8,128)(2,1)S(1)} %fusion.95), channel_id=1, source_target_pairs={{0,2},{2,0},{1,3},{3,1},{4,6},{6,4},{5,7},{7,5},{8,10},{10,8},{9,1... | collective-permute-start | bytes 393224 | tf_op jit(solution)/shard_map/ppermute | solution.py:288
  140.0 10.4 %collective-permute-start.1 = (bf16[64,1024]{1,0:T(8,128)(2,1)S(1)}, bf16[64,1024]{1,0:T(8,128)(2,1)S(1)}, u32[]{:S(2)}, u32[]{:S(2)}) collective-permute-start(bf16[64,1024]{1,0:T(8,128)(2,1)S(1)} %fusion.97), channel_id=1, source_target_pairs={{0,2},{2,0},{1,3},{3,1},{4,6},{6,4},{5,7},{7,5},{8,10},{10,8},{9,1... | collective-permute-start | bytes 393224 | tf_op jit(solution)/shard_map/ppermute | solution.py:288
  150.4 0.8 copy-start.25
  151.1 0.7 copy-start.24
  151.9 12.4 %copy-start.1 = (bf16[1792,512]{1,0:T(8,128)(2,1)S(1)}, bf16[1792,512]{1,0:T(8,128)(2,1)}, u32[]{:S(2)}) copy-start(bf16[1792,512]{1,0:T(8,128)(2,1)} %param.17) | copy-start | bytes 5505028
Sparse Core Ops, SparseCore 0:
  89.9 17.8 all-gather.1

commit v3 on v2

--- a/solution.py
+++ b/solution.py
@@ -105,6 +105,218 @@
     )(*[array for array, _, _ in items])
 
 
+def expert_stage(rows, low_sent, right, route, gate, up, down):
+    count, depth, ffw = gate.shape
+    total = rows.shape[0]
+    half = total // 2
+    cols = down.shape[2]
+    rank = right.shape[2]
+    sources = low_sent.shape[0]
+    block = total // sources
+    tile = 256 if cols % 256 == 0 and ffw % 256 == 0 else 128
+    mesh_ids = pl.DeviceIdType.MESH
+
+    def kernel(
+        rows_ref, low_ref, right_ref, route_ref, gate_ref, up_ref, down_ref, back_ref,
+        low_got, in_weights, out_weights, whole, own, sent, got, hidden, mixture, mixed,
+        in_sem, out_sem, low_send, low_recv, pre_send, pre_recv, hid_send, hid_recv,
+        back_send, back_recv,
+    ):
+        me = lax.axis_index("expert")
+        side = lax.axis_index("tensor")
+        other = {"tensor": 1 - side}
+        peers = [lax.rem(me + offset, sources) for offset in range(1, sources)]
+
+        def load_in(e):
+            return [
+                pltpu.make_async_copy(
+                    ref.at[e], in_weights.at[e % 2, which], in_sem.at[e % 2, which]
+                )
+                for which, ref in enumerate((gate_ref, up_ref))
+            ]
+
+        def load_out(e):
+            return pltpu.make_async_copy(down_ref.at[e], out_weights.at[e % 2], out_sem.at[e % 2])
+
+        for e in range(min(2, count)):
+            for copy in load_in(e):
+                copy.start()
+        for e in range(min(2, count)):
+            load_out(e).start()
+
+        barrier = pltpu.get_barrier_semaphore()
+        for target in [other] + [{"expert": peer} for peer in peers]:
+            pl.semaphore_signal(barrier, inc=1, device_id=target, device_id_type=mesh_ids)
+        pl.semaphore_wait(barrier, sources)
+
+        low_copies = []
+        for at, peer in enumerate(peers):
+            copy = pltpu.make_async_remote_copy(
+                src_ref=low_ref.at[peer],
+                dst_ref=low_got.at[me],
+                send_sem=low_send.at[at],
+                recv_sem=low_recv.at[at],
+                device_id={"expert": peer},
+                device_id_type=mesh_ids,
+            )
+            copy.start()
+            low_copies.append(copy)
+        low_got[me] = low_ref[me]
+        mixture[...] = jnp.zeros_like(mixture)
+
+        pre_copies = [
+            pltpu.make_async_remote_copy(
+                src_ref=sent.at[e],
+                dst_ref=got.at[e],
+                send_sem=pre_send.at[e],
+                recv_sem=pre_recv.at[e],
+                device_id=other,
+                device_id_type=mesh_ids,
+            )
+            for e in range(count)
+        ]
+        hid_copies = [
+            pltpu.make_async_remote_copy(
+                src_ref=hidden.at[e, pl.ds(0, half)],
+                dst_ref=hidden.at[e, pl.ds(half, half)],
+                send_sem=hid_send.at[e],
+                recv_sem=hid_recv.at[e],
+                device_id=other,
+                device_id_type=mesh_ids,
+            )
+            for e in range(count)
+        ]
+
+        def project(e):
+            for copy in load_in(e):
+                copy.wait()
+            for which in range(2):
+
+                @pl.loop(0, ffw // tile)
+                def _(step):
+                    start = pl.multiple_of(step * tile, tile)
+                    whole[which, :, pl.ds(start, tile)] = jnp.dot(
+                        rows_ref[...],
+                        in_weights[e % 2, which, :, pl.ds(start, tile)],
+                        preferred_element_type=F32,
+                    )
+
+            if e + 2 < count:
+                for copy in load_in(e + 2):
+                    copy.start()
+            if e == 0:
+                for copy in low_copies:
+                    copy.wait()
+            low = low_got[0, pl.ds(e * total, total)].astype(F32)
+            for source in range(1, sources):
+                low = low + low_got[source, pl.ds(e * total, total)].astype(F32)
+            low = low.astype(BF16)
+            for which in range(2):
+                value = whole[which] + jnp.dot(
+                    low[:, which * rank : (which + 1) * rank],
+                    right_ref[e, which],
+                    preferred_element_type=F32,
+                )
+                own[e % 2, which] = value[:half]
+                sent[e, which] = value[half:].astype(BF16)
+            pre_copies[e].start()
+
+        def activate(e):
+            pre_copies[e].wait_recv()
+            gate_sum = own[e % 2, 0] + got[e, 0].astype(F32)
+            up_sum = own[e % 2, 1] + got[e, 1].astype(F32)
+            value = gate_sum / (1.0 + jnp.exp(-gate_sum)) * up_sum
+            hidden[e, pl.ds(0, half)] = value.astype(BF16)
+            hid_copies[e].start()
+
+        def answer(e):
+            load_out(e).wait()
+            hid_copies[e].wait_recv()
+
+            @pl.loop(0, cols // tile)
+            def _(step):
+                start = pl.multiple_of(step * tile, tile)
+                value = jnp.dot(
+                    hidden[e],
+                    out_weights[e % 2, :, pl.ds(start, tile)],
+                    preferred_element_type=F32,
+                )
+                mixture[:, pl.ds(start, tile)] += route_ref[:, e : e + 1] * value.astype(
+                    BF16
+                ).astype(F32)
+
+            if e + 2 < count:
+                load_out(e + 2).start()
+
+        for e in range(count):
+            project(e)
+            if e >= 1:
+                activate(e - 1)
+            if e >= 2:
+                answer(e - 2)
+        activate(count - 1)
+        if count >= 2:
+            answer(count - 2)
+        answer(count - 1)
+
+        for place in range(sources):
+            mixed[place] = mixture[pl.ds(place * block, block)].astype(BF16)
+        turn = side * (sources // 2)
+        back_copies = []
+        for at, peer in enumerate(peers):
+            copy = pltpu.make_async_remote_copy(
+                src_ref=mixed.at[lax.rem(peer + turn, sources)],
+                dst_ref=back_ref.at[me],
+                send_sem=back_send.at[at],
+                recv_sem=back_recv.at[at],
+                device_id={"expert": peer},
+                device_id_type=mesh_ids,
+            )
+            copy.start()
+            back_copies.append(copy)
+        back_ref[me] = mixed[lax.rem(me + turn, sources)]
+        for e in range(count):
+            pre_copies[e].wait_send()
+            hid_copies[e].wait_send()
+        for copy in back_copies:
+            copy.wait()
+
+    semaphores = pltpu.SemaphoreType.DMA
+    in_vmem = pl.BlockSpec(memory_space=pltpu.VMEM)
+    in_place = pl.BlockSpec(memory_space=pl.ANY)
+    return pl.pallas_call(
+        kernel,
+        out_shape=jax.ShapeDtypeStruct((sources, block, cols), BF16),
+        in_specs=[in_vmem] * 4 + [in_place] * 3,
+        out_specs=in_vmem,
+        scratch_shapes=[
+            pltpu.VMEM(low_sent.shape, BF16),
+            pltpu.VMEM((2, 2, depth, ffw), BF16),
+            pltpu.VMEM((2, ffw, cols), BF16),
+            pltpu.VMEM((2, total, ffw), F32),
+            pltpu.VMEM((2, 2, half, ffw), F32),
+            pltpu.VMEM((count, 2, half, ffw), BF16),
+            pltpu.VMEM((count, 2, half, ffw), BF16),
+            pltpu.VMEM((count, total, ffw), BF16),
+            pltpu.VMEM((total, cols), F32),
+            pltpu.VMEM((sources, block, cols), BF16),
+            semaphores((2, 2)),
+            semaphores((2,)),
+            semaphores((sources - 1,)),
+            semaphores((sources - 1,)),
+            semaphores((count,)),
+            semaphores((count,)),
+            semaphores((count,)),
+            semaphores((count,)),
+            semaphores((sources - 1,)),
+            semaphores((sources - 1,)),
+        ],
+        compiler_params=pltpu.CompilerParams(
+            collective_id=5, has_side_effects=True, vmem_limit_bytes=44 << 20
+        ),
+    )(rows, low_sent, right, route, gate, up, down)
+
+
 def shards(
     inputs,
     attn_gain,
@@ -263,41 +475,35 @@
     low = low.astype(BF16).reshape(slots_here, total_rows, 2 * rank)
     low_sent = jnp.einsum("es,snq->enq", serves, low, preferred_element_type=F32).astype(BF16)
     low_sent = low_sent.reshape(shard_count, experts_here * total_rows, 2 * rank)
-    low_got = exchange([(low_sent, ("expert",), "scatter")], 3)[0]
-    low_own = jnp.sum(low_got.astype(F32), axis=0).astype(BF16)
-    low_own = low_own.reshape(experts_here, total_rows, 2, rank)
-
-    swap = [(0, 1), (1, 0)]
-    mixture = jnp.zeros((total_rows, part_cols), F32)
-    for expert in range(experts_here):
-        partial = [
-            jnp.dot(routed_in, weight[expert], preferred_element_type=F32)
-            + jnp.dot(
-                low_own[expert, :, which], right_full[expert, which], preferred_element_type=F32
-            )
-            for which, weight in enumerate((gate_weight, up_weight))
-        ]
-        if paired:
-            half_rows = total_rows // 2
-            sent = jnp.concatenate([value[half_rows:].astype(BF16) for value in partial], axis=1)
-            got = lax.ppermute(sent, "tensor", swap).astype(F32)
-            gate = partial[0][:half_rows] + got[:, :ffw]
-            up = partial[1][:half_rows] + got[:, ffw:]
-            hidden = (jax.nn.silu(gate) * up).astype(BF16)
-            hidden = jnp.concatenate(
-                (hidden, lax.ppermute(hidden, "tensor", swap)), axis=0
-            )
-        else:
+    if paired:
+        returned = expert_stage(
+            routed_in, low_sent, right_full, route_here, gate_weight, up_weight, down_weight
+        )
+    else:
+        low_got = exchange([(low_sent, ("expert",), "scatter")], 3)[0]
+        low_own = jnp.sum(low_got.astype(F32), axis=0).astype(BF16)
+        low_own = low_own.reshape(experts_here, total_rows, 2, rank)
+        mixture = jnp.zeros((total_rows, part_cols), F32)
+        for expert in range(experts_here):
+            partial = [
+                jnp.dot(routed_in, weight[expert], preferred_element_type=F32)
+                + jnp.dot(
+                    low_own[expert, :, which],
+                    right_full[expert, which],
+                    preferred_element_type=F32,
+                )
+                for which, weight in enumerate((gate_weight, up_weight))
+            ]
             summed = lax.psum_scatter(
                 jnp.concatenate(partial, axis=1), "tensor", scatter_dimension=0, tiled=True
             )
             hidden = (jax.nn.silu(summed[:, :ffw]) * summed[:, ffw:]).astype(BF16)
             hidden = lax.all_gather(hidden, "tensor", axis=0, tiled=True)
-        answered = jnp.dot(hidden, down_weight[expert], preferred_element_type=F32).astype(BF16)
-        mixture = mixture + route_here[:, expert : expert + 1] * answered.astype(F32)
-
-    returned = turned(mixture.astype(BF16).reshape(shard_count, batch, part_cols))
-    returned = exchange([(returned, ("expert",), "scatter")], 4)[0]
+            answered = jnp.dot(hidden, down_weight[expert], preferred_element_type=F32)
+            weight = route_here[:, expert : expert + 1]
+            mixture = mixture + weight * answered.astype(BF16).astype(F32)
+        returned = mixture.astype(BF16).reshape(shard_count, batch, part_cols)
+        returned = exchange([(returned, ("expert",), "scatter")], 4)[0]
     outputs = (middle_wide + jnp.sum(returned.astype(F32), axis=0)).astype(BF16)
     return outputs.reshape(steps, rows_here, part_cols)
 

time: 172 us -> 147 us (0.85)
  Pallas kernels: 56.1 us -> 90.9 us
  matrix products: 36.2 us -> 7.66 us
  waiting for transfers between devices: 29.4 us -> 12.9 us
  starting transfers between devices: 13.7 us -> 6.35 us
  local copies, waits for them, and re-layouts: 15.4 us -> 8.65 us
    pallas_call x0 -> x1, Pallas kernels: none -> 59.5 us  [expert_stage(): pl.pallas_call(kernel, out_shape=jax.ShapeDtypeStruct((sources, block, co...]
    dot_general x20 -> x0, matrix products: 31.8 us -> none  [the longest x8 25 us: shards(): jnp.dot(routed_in, weight[expert], preferred_element_type=F32)]
    pallas_call x5 -> x3, Pallas kernels: 56.1 us -> 31.3 us  [exchange(): pl.pallas_call(kernel, out_shape=[jax.ShapeDtypeStruct(shape, array.dtype...]
    ppermute x8 -> x0, waiting for transfers between devices: 24.7 us -> none  [the longest x4 18.8 us: shards(): got = lax.ppermute(sent, 'tensor', swap).astype(F32)]
    all_gather x1, waiting for transfers between devices: 4.67 us -> 12.9 us  [shards(): right_full = lax.all_gather(right_own, ('dp', 'tensor'), axis=3, tiled=True)]
    ppermute x8 -> x0, starting transfers between devices: 7.31 us -> none  [the longest x4 4.35 us: shards(): got = lax.ppermute(sent, 'tensor', swap).astype(F32)]
    slice x11 -> x0, local copies, waits for them, and re-layouts: 5.77 us -> none  [the longest x1 4.7 us: shards(): right_full[expert, which]]
    dot_general x1, matrix products: 1.11 us -> 3.16 us  [shards(): jnp.einsum('nd,sxdr->snxr', routed_in, pool_left, preferred_element_type=...]
  transfers between devices with their start and end apart: 10 -> 2, of which waited for: 5 -> 1; matrix products, arithmetic and copies ran while one was open for 23% -> 7% of each run, Pallas kernels for 26% -> 22%
where the time goes in v3:
time: 147 us; the launch traced here: 145 us
  Pallas kernels  90.9 us (62%)
  between operations  13.8 us (9%)
  waiting for transfers between devices  12.9 us (9%)
  local copies, waits for them, and re-layouts  8.65 us (6%)
  matrix products  7.66 us (5%)
  starting transfers between devices  6.35 us (4%)
  other arithmetic  4.81 us (3%)
    pallas_call x1, Pallas kernels, expert_stage(): pl.pallas_call(kernel, out_shape=jax.ShapeDtypeStruct((sources, block, co...  59.5 us
    pallas_call x3, Pallas kernels, exchange(): pl.pallas_call(kernel, out_shape=[jax.ShapeDtypeStruct(shape, array.dtype...  31.3 us
    all_gather x1, waiting for transfers between devices, shards(): right_full = lax.all_gather(right_own, ('dp', 'tensor'), axis=3, tiled=True)  12.9 us
    all_to_all x1, starting transfers between devices, shards(): lax.all_to_all(right_sent, 'expert', split_axis=0, concat_axis=0, tiled=T...  6.32 us
    reshape x2, local copies, waits for them, and re-layouts, shards(): right_sent.reshape(shard_count, experts_here, 2, rank, piece_cols)  3.84 us
    dot_general x1, matrix products, shards(): jnp.einsum('nd,sxdr->snxr', routed_in, pool_left, preferred_element_type=...  3.16 us
  transfers between devices with their start and end apart: 2, of which 1 were waited for; matrix products, arithmetic and copies ran while one was open for 7% of the time, Pallas kernels for 22%

profile of v3, /device:TPU:0, one launch (start us, length us, event | category | flops | bytes accessed | tf_op | source)
XLA Modules:
  0.0 145.0 jit_solution(1029348770380758636)
XLA Ops:
  6.5 1.2 constant_dynamic-slice_fusion
  7.8 1.3 convolution_convert_fusion
  9.1 1.2 reshape.141
  10.2 2.7 %copy.108 = bf16[4,4,2,64,256]{4,1,3,2,0:T(4,128)(2,1)} copy(bf16[4,4,2,64,256]{4,1,0,3,2:T(4,128)(2,1)} %reshape.141) | data formatting | bytes 2097152 | tf_op jit(solution)/shard_map/reshape | solution.py:362
  12.9 6.3 %all-to-all-start = ((bf16[4,4,2,64,256]{4,1,3,2,0:T(4,128)(2,1)}), bf16[4,4,2,64,256]{4,1,3,2,0:T(4,128)(2,1)}, u32[]{:S(2)}, u32[]{:S(2)}) async-start(bf16[4,4,2,64,256]{4,1,3,2,0:T(4,128)(2,1)} %copy.108), calls=%async_computation | async-start | bytes 2097152 | tf_op jit(solution)/shard_map/all_to_all | solution.py:363
  19.3 0.1 multiply_reduce_fusion
  19.5 0.1 rsqrt.15
  19.6 0.1 dynamic_slice.19
  19.6 0.5 fusion.10.refs_0_
  20.1 4.3 %shard_map.145 = f32[2,32,512]{2,1,0:T(8,128)S(1)} custom-call(f32[32,512]{1,0:T(8,128)S(1)} %fusion.10.refs_0_), custom_call_target="tpu_custom_call" | custom-call | tf_op jit(solution)/shard_map/pallas_call | solution.py:94
  24.5 0.4 fusion.35
  24.9 0.1 select_reduce_fusion
  25.0 0.2 reduce-precision_convert_fusion.1
  25.2 0.2 fusion.31
  25.6 0.1 pad_maximum_fusion
  25.8 4.1 %shard_map.146 = f32[2,32,384]{2,1,0:T(8,128)S(1)} custom-call(f32[32,384]{1,0:T(8,128)S(1)} %reshape.135.refs_0_), custom_call_target="tpu_custom_call" | custom-call | tf_op jit(solution)/shard_map/pallas_call | solution.py:94
  30.0 0.1 fusion.50
  30.2 0.1 copy.121
  30.2 0.1 multiply_reduce_fusion.2
  30.3 0.1 select_reduce_fusion.1
  30.5 0.1 dynamic_slice.20
  30.6 0.1 eq.34
  30.7 0.1 copy.103
  30.7 0.1 copy.120
  30.8 0.1 fusion.48
  31.0 0.1 copy.119
  31.2 0.1 copy.99
  31.2 0.1 fusion.25
  31.4 0.1 fusion.30
  31.5 1.6 %fusion.8 = (f32[32]{0:T(128)S(1)}, bf16[32,1792]{1,0:T(8,128)(2,1)S(1)}) fusion(bf16[32,256]{1,0:T(8,128)(2,1)S(1)} %bitcast.77, bf16[256,1792]{1,0:T(8,128)(2,1)} %param.18, bf16[32,3584]{1,0:T(8,128)(2,1)S(1)} %bitcast.74, s32[]{:T(128)S(6)} %select_n.58), kind=kOutput, calls=%fused_computation.20 | convolution fusion | flops 29704160 | bytes 1163396 | tf_op jit(solution)/shard_map/dot_general | solution.py:430
  33.1 0.2 fusion.7
  33.3 0.1 broadcast_in_dim.91
  33.4 0.1 pad_maximum_fusion.2.refs_0_
  33.5 22.9 %shard_map.147 = (f32[8,32,128]{2,1,0:T(8,128)S(1)}, bf16[4,32,1792]{2,1,0:T(8,128)(2,1)S(1)}) custom-call(f32[32,128]{1,0:T(8,128)S(1)} %pad_maximum_fusion.2.refs_0_, bf16[32,1792]{1,0:T(8,128)(2,1)S(1)} %get-tuple-element.28.refs_1_), custom_call_target="tpu_custom_call" | custom-call | tf_op jit(solution)/shard_map/pallas_call | solution.py:94
  56.5 1.9 %reduce_sum.143 = bf16[4,2,64,256]{3,0,2,1:T(4,128)(2,1)S(1)} reduce(bf16[4,4,2,64,256]{4,1,3,2,0:T(4,128)(2,1)} %all-to-all-done, bf16[]{:T(256)} %constant.47.clone.1), dimensions={0}, to_apply=%region_15.16 | reduce | flops 393216 | bytes 1310722 | tf_op jit(solution)/shard_map/reduce_sum | solution.py:364
  58.4 0.7 copy.110
  59.2 0.2 fusion.24
  59.4 0.2 fusion.2.rows_ref
  59.6 3.2 %convolution_convert_fusion.2 = bf16[128,8,2,64]{0,3,2,1:T(8,128)(2,1)S(1)} fusion(bf16[8,2,1792,64]{2,3,1,0:T(8,128)(2,1)} %param.27, bf16[128,1792]{1,0:T(8,128)(2,1)S(1)} %fusion.2.rows_ref), kind=kOutput, calls=%fused_computation.4 | convolution fusion | flops 469893120 | bytes 4390912 | tf_op jit(solution)/shard_map/nd,sxdr->snxr/dot_general | solution.py:474
  62.7 0.2 copy.105
  62.9 0.4 convolution_convert_fusion.1
  63.3 0.1 copy.106
  63.5 0.2 fusion.47
  63.7 0.1 fusion.28.route_ref
  63.8 12.9 %all-gather.2.cloned.1.call-done.right_ref = bf16[4,2,64,1024]{3,2,1,0:T(8,128)(2,1)} async-done(((bf16[4,2,64,256]{3,2,1,0:T(8,128)(2,1)}), bf16[4,2,64,1024]{3,2,1,0:T(8,128)(2,1)}) %all-gather.2.cloned.1.call-update) | async-done | bytes 1048592 | tf_op jit(solution)/shard_map/all_gather | solution.py:365
  76.7 1.2 copy-done.1
  77.9 59.5 %shard_map.148 = bf16[4,32,1792]{2,1,0:T(8,128)(2,1)S(1)} custom-call(bf16[128,1792]{1,0:T(8,128)(2,1)S(1)} %fusion.2.rows_ref, bf16[4,512,128]{2,1,0:T(8,128)(2,1)S(1)} %bitcast.69, bf16[4,2,64,1024]{3,2,1,0:T(8,128)(2,1)S(1)} %copy-done.1, f32[128,4]{1,0:T(8,128)S(1)} %fusion.28.route_ref, bf16[4,1792,1024]{2,1,0:T(8,128)(2,1)} %gate_ref.1, ...), custom_call_target="tpu_custom_call" | custom-call | tf_op jit(solution)/shard_map/pallas_call | solution.py:287
  137.5 0.7 fusion.9
  (53 shorter events, 0.9 us)
Async XLA Ops:
  6.5 13.1 %copy-start = (bf16[1792,512]{1,0:T(8,128)(2,1)S(1)}, bf16[1792,512]{1,0:T(8,128)(2,1)}, u32[]{:S(2)}) copy-start(bf16[1792,512]{1,0:T(8,128)(2,1)} %param.17) | copy-start | bytes 5505028
  7.8 11.6 %copy-start.3 = (bf16[2,16,3584]{2,1,0:T(8,128)(2,1)S(1)}, bf16[2,16,3584]{2,1,0:T(8,128)(2,1)}, u32[]{:S(2)}) copy-start(bf16[2,16,3584]{2,1,0:T(8,128)(2,1)} %param.15) | copy-start | bytes 688132
  7.8 11.8 %copy-start.6 = (f32[3584]{0:T(1024)S(1)}, f32[3584]{0:T(1024)}, u32[]{:S(2)}) copy-start(f32[3584]{0:T(1024)} %param.16) | copy-start | bytes 43012
  10.2 14.2 %copy-start.9 = (s32[16]{0:T(128)S(1)}, s32[16]{0:T(128)}, u32[]{:S(2)}) copy-start(s32[16]{0:T(128)} %param.20) | copy-start | bytes 196
  10.2 14.3 %copy-start.2 = (bf16[16,128,256]{2,1,0:T(8,128)(2,1)S(1)}, bf16[16,128,256]{2,1,0:T(8,128)(2,1)}, u32[]{:S(2)}) copy-start(bf16[16,128,256]{2,1,0:T(8,128)(2,1)} %param.19) | copy-start | bytes 3145732
  12.9 43.6 %all-to-all-start = ((bf16[4,4,2,64,256]{4,1,3,2,0:T(4,128)(2,1)}), bf16[4,4,2,64,256]{4,1,3,2,0:T(4,128)(2,1)}, u32[]{:S(2)}, u32[]{:S(2)}) async-start(bf16[4,4,2,64,256]{4,1,3,2,0:T(4,128)(2,1)} %copy.108), calls=%async_computation | async-start | bytes 2097152 | tf_op jit(solution)/shard_map/all_to_all | solution.py:363
  19.2 11.2 %copy-start.7 = (f32[3584]{0:T(1024)S(1)}, f32[3584]{0:T(1024)}, u32[]{:S(2)}) copy-start(f32[3584]{0:T(1024)} %param.21) | copy-start | bytes 43012
  19.2 11.3 %copy-start.5 = (s32[2,16,8]{1,2,0:T(8,128)S(1)}, s32[2,16,8]{1,2,0:T(8,128)}, u32[]{:S(2)}) copy-start(s32[2,16,8]{1,2,0:T(8,128)} %param.23) | copy-start | bytes 3076
  19.2 57.5 %all-gather.2.cloned.1.call-start = ((), (), s32[]{:S(2)}) async-start(), calls=%async_computation.1 | async-start | bytes 1310720 | tf_op jit(solution)/shard_map/all_gather | solution.py:365
  19.6 13.4 %copy-start.4 = (bf16[3584,16]{0,1:T(8,128)(2,1)S(1)}, bf16[3584,16]{0,1:T(8,128)(2,1)}, u32[]{:S(2)}) copy-start(bf16[3584,16]{0,1:T(8,128)(2,1)} %param.22) | copy-start | bytes 344068
  59.6 3.4 %copy-start.8 = (s32[16]{0:T(128)S(1)}, s32[16]{0:T(128)}, u32[]{:S(2)}) copy-start(s32[16]{0:T(128)} %param.29) | copy-start | bytes 196
  76.7 1.2 copy-start.1
Sparse Core Ops, SparseCore 0:
  59.3 17.3 all-gather.1

commit v4 on v3

--- a/solution.py
+++ b/solution.py
@@ -21,7 +21,7 @@
     return terms
 
 
-def exchange(items, collective_id):
+def exchange(items, collective_id, group=None):
     sizes = [[lax.axis_size(axis) for axis in axes] for _, axes, _ in items]
     counts = []
     for dims in sizes:
@@ -29,39 +29,43 @@
         for dim in dims:
             count *= dim
         counts.append(count)
-    greeted = max(range(len(items)), key=lambda i: counts[i])
+    greeted = group or items[max(range(len(items)), key=lambda i: counts[i])][1]
+    greeted_sizes = [lax.axis_size(axis) for axis in greeted]
+    greeted_count = 1
+    for dim in greeted_sizes:
+        greeted_count *= dim
 
     def kernel(*refs):
         number = len(items)
         sources, targets = refs[:number], refs[number : 2 * number]
         sends, receives = refs[2 * number : 3 * number], refs[3 * number : 4 * number]
 
-        def own(which):
+        def own(axes, dims):
             place = 0
-            for axis, dim in zip(items[which][1], sizes[which]):
+            for axis, dim in zip(axes, dims):
                 place = place * dim + lax.axis_index(axis)
             return place
 
-        def device(which, place):
+        def device(axes, dims, place):
             found = {}
-            for axis, dim in reversed(list(zip(items[which][1], sizes[which]))):
+            for axis, dim in reversed(list(zip(axes, dims))):
                 found[axis] = lax.rem(place, dim)
                 place = place // dim
             return found
 
         barrier = pltpu.get_barrier_semaphore()
-        me = own(greeted)
-        for offset in range(1, counts[greeted]):
+        me = own(greeted, greeted_sizes)
+        for offset in range(1, greeted_count):
             pl.semaphore_signal(
                 barrier,
                 inc=1,
-                device_id=device(greeted, lax.rem(me + offset, counts[greeted])),
+                device_id=device(greeted, greeted_sizes, lax.rem(me + offset, greeted_count)),
                 device_id_type=pl.DeviceIdType.MESH,
             )
-        pl.semaphore_wait(barrier, counts[greeted] - 1)
+        pl.semaphore_wait(barrier, greeted_count - 1)
         copies = []
         for which in range(number):
-            me, count = own(which), counts[which]
+            me, count = own(items[which][1], sizes[which]), counts[which]
             for offset in range(1, count):
                 peer = lax.rem(me + offset, count)
                 source = sources[which]
@@ -72,13 +76,13 @@
                     dst_ref=targets[which].at[me],
                     send_sem=sends[which].at[offset - 1],
                     recv_sem=receives[which].at[offset - 1],
-                    device_id=device(which, peer),
+                    device_id=device(items[which][1], sizes[which], peer),
                     device_id_type=pl.DeviceIdType.MESH,
                 )
                 copy.start()
                 copies.append(copy)
         for which in range(number):
-            me = own(which)
+            me = own(items[which][1], sizes[which])
             if items[which][2] == "scatter":
                 targets[which][me] = sources[which][me]
             else:
@@ -359,10 +363,7 @@
     right_sent = jnp.einsum(
         "es,sxrf->exrf", serves, right_piece, preferred_element_type=F32
     ).astype(BF16)
-    right_sent = right_sent.reshape(shard_count, experts_here, 2, rank, piece_cols)
-    right_got = lax.all_to_all(right_sent, "expert", split_axis=0, concat_axis=0, tiled=True)
-    right_own = jnp.sum(right_got.astype(F32), axis=0).astype(BF16)
-    right_full = lax.all_gather(right_own, ("dp", "tensor"), axis=3, tiled=True)
+    right_sent = right_sent.reshape(shard_count, experts_here * 2 * rank, piece_cols)
 
     chosen = jnp.any(
         expert_ids.reshape(batch, -1)[:, :, None]
@@ -379,7 +380,18 @@
         token_cols.astype(F32) * lax.rsqrt(square_mean + EPS) * gain_piece
     ).astype(BF16)
     projected = jnp.dot(normed_cols, qkv_weight, preferred_element_type=F32)
-    projected = jnp.sum(exchange([(projected, ("tensor",), "gather")], 0)[0], axis=0)
+    projected_all, right_got = exchange(
+        [
+            (projected, ("tensor",), "gather"),
+            (right_sent, ("expert",), "scatter"),
+        ],
+        0,
+        ("expert", "tensor"),
+    )
+    projected = jnp.sum(projected_all, axis=0)
+    right_own = jnp.sum(right_got.astype(F32), axis=0).astype(BF16)
+    right_own = right_own.reshape(experts_here, 2, rank, piece_cols)
+    right_full = lax.all_gather(right_own, ("dp", "tensor"), axis=3, tiled=True)
     queries = projected[:, :lat].astype(BF16).reshape(steps, rows_here, lat)
     fresh = projected[:, lat:].astype(BF16).reshape(steps, rows_here, lat)
 

time: 147 us -> 138 us (0.939)
  Pallas kernels: 90.9 us -> 104 us
  waiting for transfers between devices: 12.9 us -> 0.04 us
  starting transfers between devices: 6.35 us -> 0.01 us
  local copies, waits for them, and re-layouts: 8.65 us -> 5.26 us
    pallas_call x3, Pallas kernels: 31.3 us -> 46.8 us  [exchange(): pl.pallas_call(kernel, out_shape=[jax.ShapeDtypeStruct(shape, array.dtype...]
    all_gather x1, waiting for transfers between devices: 12.9 us -> 0.02 us  [shards(): right_full = lax.all_gather(right_own, ('dp', 'tensor'), axis=3, tiled=True)]
    all_to_all x1 -> x0, starting transfers between devices: 6.32 us -> none  [shards(): lax.all_to_all(right_sent, 'expert', split_axis=0, concat_axis=0, tiled=T...]
    reshape x2 -> x0, local copies, waits for them, and re-layouts: 3.84 us -> none  [shards(): right_sent.reshape(shard_count, experts_here, 2, rank, piece_cols)]
    pallas_call x1, Pallas kernels: 59.5 us -> 56.9 us  [expert_stage(): pl.pallas_call(kernel, out_shape=jax.ShapeDtypeStruct((sources, block, co...]
    dot_general x1, matrix products: 3.16 us -> 1.11 us  [shards(): jnp.einsum('nd,sxdr->snxr', routed_in, pool_left, preferred_element_type=...]
  transfers between devices with their start and end apart: 2 -> 1, of which waited for: 1 -> 0; matrix products, arithmetic and copies ran while one was open for 7% -> 7% of each run, Pallas kernels for 22% -> 16%
where the time goes in v4:
time: 138 us; the launch traced here: 137 us
  Pallas kernels  104 us (75%)
  between operations  13.8 us (10%)
  matrix products  8.21 us (6%)
  other arithmetic  6.22 us (5%)
  local copies, waits for them, and re-layouts  5.26 us (4%)
    pallas_call x1, Pallas kernels, expert_stage(): pl.pallas_call(kernel, out_shape=jax.ShapeDtypeStruct((sources, block, co...  56.9 us
    pallas_call x3, Pallas kernels, exchange(): pl.pallas_call(kernel, out_shape=[jax.ShapeDtypeStruct(shape, array.dtype...  46.8 us
  transfers between devices with their start and end apart: 1, of which 0 were waited for; matrix products, arithmetic and copies ran while one was open for 7% of the time, Pallas kernels for 16%

profile of v4, /device:TPU:0, one launch (start us, length us, event | category | flops | bytes accessed | tf_op | source)
XLA Modules:
  0.0 137.3 jit_solution(3506861133560413578)
XLA Ops:
  6.6 1.2 multiply_reduce_fusion
  7.8 0.1 rsqrt.15
  7.9 1.1 constant_dynamic-slice_fusion
  9.0 1.2 convolution_convert_fusion
  10.2 0.3 copy.88
  10.6 0.1 dynamic_slice.19
  10.7 0.5 fusion.10.refs_0_
  11.1 24.2 %shard_map.145 = (f32[2,32,512]{2,1,0:T(8,128)S(1)}, bf16[4,512,256]{2,1,0:T(8,128)(2,1)S(1)}) custom-call(f32[32,512]{1,0:T(8,128)S(1)} %fusion.10.refs_0_, bf16[4,512,256]{2,1,0:T(8,128)(2,1)S(1)} %bitcast.67), custom_call_target="tpu_custom_call" | custom-call | tf_op jit(solution)/shard_map/pallas_call | solution.py:98
  35.3 1.0 copy-done.2
  36.3 2.2 %reduce_sum.143 = bf16[512,256]{1,0:T(8,128)(2,1)} reduce(bf16[4,512,256]{2,1,0:T(8,128)(2,1)} %copy-done.2, bf16[]{:T(256)} %constant.47.clone.1), dimensions={0}, to_apply=%region_15.16 | reduce | flops 393216 | bytes 1310722 | tf_op jit(solution)/shard_map/reduce_sum | solution.py:392
  38.6 0.1 broadcast_compare_fusion
  38.7 1.6 %fusion.35 = f32[16,2,128]{2,1,0:T(2,128)S(1)} fusion(bf16[16,128,256]{2,1,0:T(8,128)(2,1)} %param.19, bf16[2,16,256]{2,1,0:T(8,128)(2,1)S(1)} %bitcast.76), kind=kOutput, calls=%fused_computation.65 | convolution fusion | flops 2097152 | bytes 1081344 | tf_op jit(solution)/shard_map/sbl,bpl->bsp/dot_general | solution.py:401
  40.3 0.1 select_reduce_fusion
  40.4 0.2 reduce-precision_convert_fusion.1
  40.6 1.5 %fusion.31 = f32[16,6,256]{2,1,0:T(8,128)S(1)} fusion(bf16[16,128,256]{2,1,0:T(8,128)(2,1)} %param.19, bf16[16,6,128]{2,0,1:T(8,128)(2,1)S(1)} %pad_maximum_fusion.1), kind=kOutput, calls=%fused_computation.54 | convolution fusion | flops 6291456 | bytes 1171456 | tf_op jit(solution)/shard_map/bmp,bpl->bml/dot_general | solution.py:406
  42.1 0.1 broadcast_in_dim.51
  42.3 0.1 pad_maximum_fusion
  42.4 4.1 %shard_map.146 = f32[2,32,384]{2,1,0:T(8,128)S(1)} custom-call(f32[32,384]{1,0:T(8,128)S(1)} %reshape.139.refs_0_), custom_call_target="tpu_custom_call" | custom-call | tf_op jit(solution)/shard_map/pallas_call | solution.py:98
  46.6 0.1 fusion.50
  46.8 0.1 copy.114
  46.9 0.1 multiply_reduce_fusion.2
  47.0 0.1 select_reduce_fusion.1
  47.1 0.1 dynamic_slice.21
  47.2 0.1 eq.37
  47.3 0.1 copy.101
  47.4 0.1 copy.113
  47.5 0.1 fusion.48
  47.6 0.1 multiply_reduce_fusion.1
  47.6 0.1 copy.112
  47.8 0.1 copy.97
  47.9 0.1 fusion.25
  48.0 0.1 fusion.30
  48.1 1.7 %fusion.8 = (f32[32]{0:T(128)S(1)}, bf16[32,1792]{1,0:T(8,128)(2,1)S(1)}) fusion(bf16[32,256]{1,0:T(8,128)(2,1)S(1)} %bitcast.77, bf16[256,1792]{1,0:T(8,128)(2,1)} %param.18, bf16[32,3584]{1,0:T(8,128)(2,1)S(1)} %bitcast.74, s32[]{:T(128)S(6)} %select_n.58), kind=kOutput, calls=%fused_computation.20 | convolution fusion | flops 29704160 | bytes 1163396 | tf_op jit(solution)/shard_map/dot_general | solution.py:442
  49.9 0.2 fusion.7
  50.1 0.1 broadcast_in_dim.91
  50.2 0.1 pad_maximum_fusion.2.refs_0_
  50.3 18.5 %shard_map.147 = (f32[8,32,128]{2,1,0:T(8,128)S(1)}, bf16[4,32,1792]{2,1,0:T(8,128)(2,1)S(1)}) custom-call(f32[32,128]{1,0:T(8,128)S(1)} %pad_maximum_fusion.2.refs_0_, bf16[32,1792]{1,0:T(8,128)(2,1)S(1)} %get-tuple-element.32.refs_1_), custom_call_target="tpu_custom_call" | custom-call | tf_op jit(solution)/shard_map/pallas_call | solution.py:98
  68.9 0.2 fusion.24
  69.1 0.2 fusion.2.rows_ref
  69.3 1.1 convolution_convert_fusion.2
  70.4 0.2 copy.103
  70.6 0.4 convolution_convert_fusion.1
  71.1 0.1 copy.104
  71.2 0.2 fusion.47
  71.4 0.1 fusion.28.route_ref
  71.6 1.2 copy-done.1
  72.8 56.9 %shard_map.148 = bf16[4,32,1792]{2,1,0:T(8,128)(2,1)S(1)} custom-call(bf16[128,1792]{1,0:T(8,128)(2,1)S(1)} %fusion.2.rows_ref, bf16[4,512,128]{2,1,0:T(8,128)(2,1)S(1)} %bitcast.68, bf16[4,2,64,1024]{3,2,1,0:T(8,128)(2,1)S(1)} %copy-done.1, f32[128,4]{1,0:T(8,128)S(1)} %fusion.28.route_ref, bf16[4,1792,1024]{2,1,0:T(8,128)(2,1)} %gate_ref.1, ...), custom_call_target="tpu_custom_call" | custom-call | tf_op jit(solution)/shard_map/pallas_call | solution.py:291
  129.8 0.7 fusion.9
  (51 shorter events, 0.7 us)
Async XLA Ops:
  6.5 4.1 %copy-start = (bf16[1792,512]{1,0:T(8,128)(2,1)S(1)}, bf16[1792,512]{1,0:T(8,128)(2,1)}, u32[]{:S(2)}) copy-start(bf16[1792,512]{1,0:T(8,128)(2,1)} %param.17) | copy-start | bytes 5505028
  6.5 4.1 %copy-start.4 = (bf16[2,16,3584]{2,1,0:T(8,128)(2,1)S(1)}, bf16[2,16,3584]{2,1,0:T(8,128)(2,1)}, u32[]{:S(2)}) copy-start(bf16[2,16,3584]{2,1,0:T(8,128)(2,1)} %param.15) | copy-start | bytes 688132
  6.5 4.0 %copy-start.7 = (f32[3584]{0:T(1024)S(1)}, f32[3584]{0:T(1024)}, u32[]{:S(2)}) copy-start(f32[3584]{0:T(1024)} %param.16) | copy-start | bytes 43012
  6.5 65.0 %all-gather.2.cloned.1.call-start = ((), (), s32[]{:S(2)}) async-start(), calls=%async_computation | async-start | bytes 1310720 | tf_op jit(solution)/shard_map/all_gather | solution.py:394
  10.2 28.4 %copy-start.10 = (s32[16]{0:T(128)S(1)}, s32[16]{0:T(128)}, u32[]{:S(2)}) copy-start(s32[16]{0:T(128)} %param.20) | copy-start | bytes 196
  11.1 36.0 %copy-start.8 = (f32[3584]{0:T(1024)S(1)}, f32[3584]{0:T(1024)}, u32[]{:S(2)}) copy-start(f32[3584]{0:T(1024)} %param.21) | copy-start | bytes 43012
  11.1 36.0 %copy-start.6 = (s32[2,16,8]{1,2,0:T(8,128)S(1)}, s32[2,16,8]{1,2,0:T(8,128)}, u32[]{:S(2)}) copy-start(s32[2,16,8]{1,2,0:T(8,128)} %param.23) | copy-start | bytes 3076
  35.3 1.0 copy-start.2
  36.3 13.5 %copy-start.5 = (bf16[3584,16]{0,1:T(8,128)(2,1)S(1)}, bf16[3584,16]{0,1:T(8,128)(2,1)}, u32[]{:S(2)}) copy-start(bf16[3584,16]{0,1:T(8,128)(2,1)} %param.22) | copy-start | bytes 344068
  47.9 21.4 %copy-start.3 = (bf16[8,2,1792,64]{2,3,1,0:T(8,128)(2,1)S(1)}, bf16[8,2,1792,64]{2,3,1,0:T(8,128)(2,1)}, u32[]{:S(2)}) copy-start(bf16[8,2,1792,64]{2,3,1,0:T(8,128)(2,1)} %param.27) | copy-start | bytes 11010052
  69.3 1.3 copy-start.9
  71.5 1.2 copy-start.1
Sparse Core Ops, SparseCore 0:
  38.7 21.8 all-gather.1
